TPU v7x, 512 devices: a whole 4x8x8 slice. The times are simulated.
512 devices in a mesh: row: 8 (over y_hi, core), col: 64 (over z, y_lo, x).
Axes of the slice: x: 4, y: 8 (y_hi: 4, y_lo: 2; y = y_hi * 2 + y_lo), z: 8, core: 2. Of those that a mesh axis runs over, the one named last changes fastest.
Arguments:
- velocity: bfloat16 [3, 64, 1280, 1024], P(None, 'col', 'row'), may hold values from -6 to 6
- lengths: int32 [64, 8], P('col'), may hold values from 1 to 160, 1024 in all within a row
- inverse_x: float32 [4, 256, 256], replicated, as said below
- inverse_y: float32 [4, 256, 256], replicated, as said below
- metric: float32 [1024], replicated, may hold values from 0.25 to 4
Outputs:
- slope_x: bfloat16 [3, 64, 1024, 1024], P(None, None, 'col', 'row')
- slope_y: bfloat16 [3, 64, 1024, 1024], P(None, None, 'col', 'row')
Inputs may be any that keep to these rules, and one draw needn't show every extreme that they name: For each plane, row index i uses its first lengths[z, i] slots; each plane's lengths sum to 1024 and their largest is 160. `inverse_x`: each block has a dominant diagonal. `inverse_y`: each block has a dominant diagonal.
All inputs are finite; a program needn't handle non-finite values.
Results may differ from a plain program's by a relative error of at most 0.001.
Values may be sent and summed in bfloat16 or wider, within the bound.
No kernel may reach another device: no remote copies, remote signals or barrier semaphores. Data moves between devices by JAX's collectives and lax.ppermute only.
A program may use at most 64 MiB of HBM per device.

v0:
```python
import jax
import jax.numpy as jnp
from jax import lax
from jax.sharding import PartitionSpec as P

YDEV = 128


A_COEF = 14.0 / 9.0
B_COEF = 1.0 / 9.0
ALPHA = 1.0 / 3.0


def source_rows(lengths, grid_rows, capacity):
    row_ends = jnp.cumsum(lengths)
    starts = row_ends - lengths
    indices = jnp.arange(grid_rows, dtype=jnp.int32)
    owners = jnp.sum((indices[:, None] >= row_ends[None, :]).astype(jnp.int32), axis=1)
    ranks_all = jnp.arange(lengths.shape[0], dtype=jnp.int32)
    start_of = jnp.sum(jnp.where(ranks_all[None, :] == owners[:, None], starts[None, :], 0), axis=1)
    return owners * capacity + indices - start_of


def explicit_part(field, along):
    extent = field.shape[along]
    widths_pad = [(0, 0)] * field.ndim
    widths_pad[along] = (2, 2)
    padded = jnp.pad(field, widths_pad)

    def offset_slice(shift):
        return lax.slice_in_dim(padded, 2 + shift, 2 + shift + extent, axis=along)

    return A_COEF / 2.0 * (offset_slice(1) - offset_slice(-1)) + B_COEF / 4.0 * (
        offset_slice(2) - offset_slice(-2)
    )


def apply_block(inverse, block_now, along):
    if along == 3:
        return jnp.einsum("cayj,ij->cayi", block_now, inverse, precision=lax.Precision.HIGHEST)
    return jnp.einsum("ij,cajx->caix", inverse, block_now, precision=lax.Precision.HIGHEST)


def block_solve(rhs, inverse, along):
    blocks = inverse.shape[0]
    width = inverse.shape[1]
    solved = []
    previous = None
    for number in range(blocks):
        block_now = lax.slice_in_dim(rhs, number * width, (number + 1) * width, axis=along)
        if previous is not None:
            head_row = lax.slice_in_dim(block_now, 0, 1, axis=along) - ALPHA * lax.slice_in_dim(
                previous, width - 1, width, axis=along
            )
            block_now = jnp.concatenate(
                [head_row, lax.slice_in_dim(block_now, 1, width, axis=along)], axis=along
            )
        previous = apply_block(inverse[number], block_now, along)
        solved.append(previous)
    result = [None] * blocks
    result[blocks - 1] = solved[blocks - 1]
    for number in range(blocks - 2, -1, -1):
        shape_col = [1] * rhs.ndim
        shape_col[along] = width
        column = inverse[number][:, width - 1].reshape(shape_col)
        following = lax.slice_in_dim(result[number + 1], 0, 1, axis=along)
        result[number] = solved[number] - ALPHA * column * following
    return jnp.concatenate(result, axis=along)


def streamwise(velocity, inverse_x):
    return block_solve(explicit_part(velocity.astype(jnp.float32), 3), inverse_x, 3).astype(
        jnp.bfloat16
    )


def wall_normal(packed, inverse_y, metric):
    return (
        metric[:, None] * block_solve(explicit_part(packed.astype(jnp.float32), 2), inverse_y, 2)
    ).astype(jnp.bfloat16)


def take_plane(values, sources):
    return jnp.take(values, sources, axis=1)


def local(velocity, lengths, inverse_x, inverse_y, metric):
    capacity = velocity.shape[2]
    row_count = lax.axis_size("row")
    grid_rows = row_count * YDEV
    sources = jax.vmap(lambda single: source_rows(single, grid_rows, capacity))(lengths)

    def compact(received):
        return jax.vmap(take_plane, in_axes=(1, 0), out_axes=1)(received, sources)

    derived_x = streamwise(velocity, inverse_x)
    moved_fields, moved_slopes = (
        lax.all_to_all(velocity, "row", split_axis=3, concat_axis=2, tiled=True),
        lax.all_to_all(derived_x, "row", split_axis=3, concat_axis=2, tiled=True),
    )
    packed_fields = compact(moved_fields)
    packed_slopes = compact(moved_slopes)
    derived_y = wall_normal(packed_fields, inverse_y, metric)
    result_x, result_y = (
        lax.all_to_all(packed_slopes, "col", split_axis=2, concat_axis=1, tiled=True),
        lax.all_to_all(derived_y, "col", split_axis=2, concat_axis=1, tiled=True),
    )
    return (result_x, result_y)


def solution(mesh):
    return jax.shard_map(
        local,
        mesh=mesh,
        in_specs=(P(None, "col", "row", None), P("col", None), P(), P(), P()),
        out_specs=(P(None, None, "col", "row"), P(None, None, "col", "row")),
        check_vma=False,
    )
```

profile of v0, /device:TPU:1, one launch (start us, length us, event | category | flops | bytes accessed | tf_op | source)
XLA Modules:
  0.0 180.8 jit_solution(11193046790337235297)
XLA Ops:
  0.6 2.8 %copy.70 = bf16[3,1,160,1024]{2,0,1,3:T(4,128)(2,1)S(1)} copy(bf16[3,1,160,1024]{3,2,1,0:T(8,128)(2,1)} %param.7) | data formatting | bytes 1966080 | tf_op args[0]
  3.5 3.3 %reshape.488 = bf16[8,2,30720]{2,1,0:T(2,128)(2,1)} reshape(bf16[1024,1,3,160]{3,2,1,0:T(4,128)(2,1)S(1)} %bitcast.153) | data formatting | bytes 1966080
  6.8 11.0 %all-to-all-start.2 = ((bf16[8,2,30720]{2,1,0:T(2,128)(2,1)}), bf16[8,2,30720]{2,1,0:T(2,128)(2,1)}, u32[]{:S(2)}, u32[]{:S(2)}) async-start(bf16[8,2,30720]{2,1,0:T(2,128)(2,1)} %reshape.488), calls=%async_computation.2 | async-start | bytes 1966080 | tf_op jit(solution)/shard_map/all_to_all | solution.py:98
  18.3 1.6 fusion.1
  25.5 1.4 copy.65
  26.9 3.3 %reshape.486 = bf16[8,2,30720]{2,1,0:T(2,128)(2,1)} reshape(bf16[1024,1,3,160]{3,2,1,0:T(4,128)(2,1)S(1)} %bitcast.150) | data formatting | bytes 1966080
  30.9 11.6 %all-to-all-done.2 = bf16[8,2,30720]{2,1,0:T(2,128)(2,1)} async-done(((bf16[8,2,30720]{2,1,0:T(2,128)(2,1)}), bf16[8,2,30720]{2,1,0:T(2,128)(2,1)}, u32[]{:S(2)}, u32[]{:S(2)}) %all-to-all-start.2) | async-done | bytes 983072 | tf_op jit(solution)/shard_map/all_to_all | solution.py:98
  42.5 5.2 %all-to-all-start = ((bf16[8,2,30720]{2,1,0:T(2,128)(2,1)}), bf16[8,2,30720]{2,1,0:T(2,128)(2,1)}, u32[]{:S(2)}, u32[]{:S(2)}) async-start(bf16[8,2,30720]{2,1,0:T(2,128)(2,1)} %reshape.486), calls=%async_computation | async-start | bytes 1966080 | tf_op jit(solution)/shard_map/all_to_all | solution.py:99
  48.0 3.8 %reshape.489 = bf16[1024,1,3,160]{3,2,1,0:T(4,128)(2,1)S(1)} reshape(bf16[8,2,30720]{2,1,0:T(2,128)(2,1)} %all-to-all-done.2) | data formatting | bytes 1966080
  53.1 6.1 %copy.84 = bf16[3,1,1280,128]{3,0,2,1:T(4,128)(2,1)S(1)} copy(bf16[3,1,1280,128]{3,2,0,1:T(8,128)(2,1)S(1)} %bitcast.156) | data formatting | bytes 1966080 | tf_op jit(solution)/shard_map/all_to_all | solution.py:98
  59.2 3.7 %gather_fusion.1 = bf16[1024,3,128]{2,1,0:T(4,128)(2,1)S(1)} fusion(bf16[1,3,1280,128]{3,1,2,0:T(4,128)(2,1)S(1)} %bitcast.159, s32[1024]{0:T(1024)S(1)} %bitcast.148), kind=kCustom, calls=%fused_computation.1.clone | custom fusion | bytes 1581056 | tf_op jit(solution)/shard_map/vmap(jit(_take))/gather | solution.py:84
  65.3 1.5 convolution_bitcast_fusion.4
  68.0 5.4 %all-to-all-done = bf16[8,2,30720]{2,1,0:T(2,128)(2,1)} async-done(((bf16[8,2,30720]{2,1,0:T(2,128)(2,1)}), bf16[8,2,30720]{2,1,0:T(2,128)(2,1)}, u32[]{:S(2)}, u32[]{:S(2)}) %all-to-all-start) | async-done | bytes 983072 | tf_op jit(solution)/shard_map/all_to_all | solution.py:99
  73.3 4.8 %reshape.487 = bf16[1024,1,3,160]{3,2,1,0:T(4,128)(2,1)} reshape(bf16[8,2,30720]{2,1,0:T(2,128)(2,1)} %all-to-all-done) | data formatting | bytes 1966080
  78.1 2.9 %copy.79 = bf16[3,1,160,8,128]{4,2,3,0,1:T(8,128)(2,1)S(1)} copy(bf16[3,1,160,8,128]{2,0,4,3,1:T(4,128)(2,1)} %bitcast.152) | data formatting | bytes 1966080 | tf_op jit(solution)/shard_map/all_to_all | solution.py:99
  81.1 7.0 %copy.85 = bf16[3,1,1280,128]{3,0,2,1:T(4,128)(2,1)} copy(bf16[3,1,1280,128]{3,2,0,1:T(8,128)(2,1)S(1)} %bitcast.157) | data formatting | bytes 1966080 | tf_op jit(solution)/shard_map/all_to_all | solution.py:99
  88.0 9.1 %gather_fusion = bf16[1024,3,128]{2,1,0:T(4,128)(2,1)} fusion(bf16[1,3,1280,128]{3,1,2,0:T(4,128)(2,1)} %bitcast.158, s32[1024]{0:T(1024)S(1)} %bitcast.149), kind=kCustom, calls=%fused_computation.clone | custom fusion | bytes 1581056 | tf_op jit(solution)/shard_map/vmap(jit(_take))/gather | solution.py:84
  97.1 6.1 %fusion.7 = bf16[3,1,1024,128]{3,0,1,2:T(4,128)(2,1)} fusion(bf16[1024,3,128]{2,1,0:T(4,128)(2,1)} %gather_fusion, pred[1024]{0:T(1024)(128)(4,1)S(1)} %get-tuple-element.17), kind=kLoop, calls=%fused_computation.23 | loop fusion | flops 393216 | bytes 1573888 | tf_op jit(solution)/shard_map/vmap()/transpose | solution.py:94
  103.2 15.1 %all-to-all-start.1 = ((bf16[3,1,1024,128]{3,0,1,2:T(4,128)(2,1)}), bf16[3,1,1024,128]{3,0,1,2:T(4,128)(2,1)S(1)}, u32[]{:S(2)}, u32[]{:S(2)}) async-start(bf16[3,1,1024,128]{3,0,1,2:T(4,128)(2,1)} %fusion.7), calls=%async_computation.1 | async-start | bytes 2097152 | tf_op jit(solution)/shard_map/all_to_all | solution.py:105
  118.4 1.7 convolution_bitcast_fusion.3
  122.5 1.4 copy.75
  123.9 21.4 %all-to-all-done.1 = bf16[3,1,1024,128]{3,0,1,2:T(4,128)(2,1)S(1)} async-done(((bf16[3,1,1024,128]{3,0,1,2:T(4,128)(2,1)}), bf16[3,1,1024,128]{3,0,1,2:T(4,128)(2,1)S(1)}, u32[]{:S(2)}, u32[]{:S(2)}) %all-to-all-start.1) | async-done | bytes 786464 | tf_op jit(solution)/shard_map/all_to_all | solution.py:105
  145.3 7.5 %all-to-all-start.3 = ((bf16[3,1,1024,128]{3,0,1,2:T(4,128)(2,1)}), bf16[3,1,1024,128]{3,0,1,2:T(4,128)(2,1)S(1)}, u32[]{:S(2)}, u32[]{:S(2)}) async-start(bf16[3,1,1024,128]{3,0,1,2:T(4,128)(2,1)} %copy.75), calls=%async_computation.3 | async-start | bytes 2097152 | tf_op jit(solution)/shard_map/all_to_all | solution.py:106
  153.9 26.0 %all-to-all-done.3 = bf16[3,1,1024,128]{3,0,1,2:T(4,128)(2,1)S(1)} async-done(((bf16[3,1,1024,128]{3,0,1,2:T(4,128)(2,1)}), bf16[3,1,1024,128]{3,0,1,2:T(4,128)(2,1)S(1)}, u32[]{:S(2)}, u32[]{:S(2)}) %all-to-all-start.3) | async-done | bytes 786464 | tf_op jit(solution)/shard_map/all_to_all | solution.py:106
  (64 shorter events, 16.1 us)
Async XLA Ops:
  3.5 14.3 %copy-start = (bf16[3,1,160,1024]{3,2,1,0:T(8,128)(2,1)S(1)}, bf16[3,1,160,1024]{3,2,1,0:T(8,128)(2,1)}, u32[]{:S(2)}) copy-start(bf16[3,1,160,1024]{3,2,1,0:T(8,128)(2,1)} %param.7) | copy-start | bytes 2949124
  6.8 35.7 %all-to-all-start.2 = ((bf16[8,2,30720]{2,1,0:T(2,128)(2,1)}), bf16[8,2,30720]{2,1,0:T(2,128)(2,1)}, u32[]{:S(2)}, u32[]{:S(2)}) async-start(bf16[8,2,30720]{2,1,0:T(2,128)(2,1)} %reshape.488), calls=%async_computation.2 | async-start | bytes 1966080 | tf_op jit(solution)/shard_map/all_to_all | solution.py:98
  19.8 1.2 copy-start.3
  26.9 3.4 %copy-start.6 = (s32[1,8]{1,0:T(1,128)S(1)}, s32[1,8]{1,0:T(1,128)}, u32[]{:S(2)}) copy-start(s32[1,8]{1,0:T(1,128)} %param.8) | copy-start | bytes 100
  26.9 3.7 %copy-start.1 = (f32[4,256,256]{2,1,0:T(8,128)S(1)}, f32[4,256,256]{2,1,0:T(8,128)}, u32[]{:S(2)}) copy-start(f32[4,256,256]{2,1,0:T(8,128)} %param.10) | copy-start | bytes 3145732
  42.5 30.8 %all-to-all-start = ((bf16[8,2,30720]{2,1,0:T(2,128)(2,1)}), bf16[8,2,30720]{2,1,0:T(2,128)(2,1)}, u32[]{:S(2)}, u32[]{:S(2)}) async-start(bf16[8,2,30720]{2,1,0:T(2,128)(2,1)} %reshape.486), calls=%async_computation | async-start | bytes 1966080 | tf_op jit(solution)/shard_map/all_to_all | solution.py:99
  103.2 42.1 %all-to-all-start.1 = ((bf16[3,1,1024,128]{3,0,1,2:T(4,128)(2,1)}), bf16[3,1,1024,128]{3,0,1,2:T(4,128)(2,1)S(1)}, u32[]{:S(2)}, u32[]{:S(2)}) async-start(bf16[3,1,1024,128]{3,0,1,2:T(4,128)(2,1)} %fusion.7), calls=%async_computation.1 | async-start | bytes 2097152 | tf_op jit(solution)/shard_map/all_to_all | solution.py:105
  118.3 2.0 %copy-start.2 = (f32[4,256,256]{2,1,0:T(8,128)S(1)}, f32[4,256,256]{2,1,0:T(8,128)}, u32[]{:S(2)}) copy-start(f32[4,256,256]{2,1,0:T(8,128)} %param.10) | copy-start | bytes 3145732
  118.3 2.0 %copy-start.4 = (f32[3,1,255,128]{2,3,0,1:T(8,128)S(1)}, f32[3,1,255,128]{2,3,0,1:T(8,128)}, u32[]{:S(2)}) copy-start(f32[3,1,255,128]{2,3,0,1:T(8,128)} %get-tuple-element.28) | copy-start | bytes 1175044
  121.5 0.8 copy-start.5
  145.3 34.6 %all-to-all-start.3 = ((bf16[3,1,1024,128]{3,0,1,2:T(4,128)(2,1)}), bf16[3,1,1024,128]{3,0,1,2:T(4,128)(2,1)S(1)}, u32[]{:S(2)}, u32[]{:S(2)}) async-start(bf16[3,1,1024,128]{3,0,1,2:T(4,128)(2,1)} %copy.75), calls=%async_computation.3 | async-start | bytes 2097152 | tf_op jit(solution)/shard_map/all_to_all | solution.py:106
where the time goes:
time: 182 us; the launch traced here: 181 us
  waiting for transfers between devices  64.3 us (35%)
  local copies, waits for them, and re-layouts  57.1 us (31%)
  starting transfers between devices  38.9 us (21%)
  other arithmetic  12.9 us (7%)
  matrix products  6.58 us (4%)
    all_to_all x1, waiting for transfers between devices, local(): lax.all_to_all(derived_y, 'col', split_axis=2, concat_axis=1, tiled=True)  26 us
    all_to_all x1, waiting for transfers between devices, local(): lax.all_to_all(packed_slopes, 'col', split_axis=2, concat_axis=1, tiled=T...  21.4 us
    unnamed x20, local copies, waits for them, and re-layouts  19.9 us
    all_to_all x1, starting transfers between devices, local(): lax.all_to_all(packed_slopes, 'col', split_axis=2, concat_axis=1, tiled=T...  15.1 us
    gather x4, local copies, waits for them, and re-layouts, take_plane(): return jnp.take(values, sources, axis=1)  13.4 us
    all_to_all x1, waiting for transfers between devices, local(): lax.all_to_all(velocity, 'row', split_axis=3, concat_axis=2, tiled=True)  11.6 us
    all_to_all x1, starting transfers between devices, local(): lax.all_to_all(velocity, 'row', split_axis=3, concat_axis=2, tiled=True)  11 us
    all_to_all x2, local copies, waits for them, and re-layouts, local(): lax.all_to_all(derived_x, 'row', split_axis=3, concat_axis=2, tiled=True)  9.91 us
  transfers between devices with their start and end apart: 4, of which 4 were waited for; matrix products, arithmetic and copies ran while one was open for 21% of the time, Pallas kernels for 0%

commit v1 on v0

v1 whole, which is shorter than its diff:
```python
import jax
import jax.numpy as jnp
from jax import lax
from jax.experimental import pallas as pl
from jax.experimental.pallas import tpu as pltpu
from jax.sharding import PartitionSpec as P

A2 = 14.0 / 9.0 / 2.0
B4 = 1.0 / 9.0 / 4.0
ALPHA = 1.0 / 3.0
F32 = jnp.float32
BF16 = jnp.bfloat16
NT = (((1,), (1,)), ((), ()))
MIB = 1 << 20


def lanes(shape):
    return lax.broadcasted_iota(jnp.int32, shape, len(shape) - 1)


def sublanes(shape):
    return lax.broadcasted_iota(jnp.int32, shape, len(shape) - 2)


def split(value):
    high = value.astype(BF16)
    return high, (value - high.astype(F32)).astype(BF16)


def roll(value, shift):
    return pltpu.roll(value, shift % value.shape[-1], value.ndim - 1)


def stencil(rows):
    return A2 * (roll(rows, 1) - roll(rows, -1)) + B4 * (roll(rows, 2) - roll(rows, -2))


def stencil_line(rows):
    width = rows.shape[-1]
    lane = lanes(rows.shape)

    def shifted(by):
        inside = lane >= by if by > 0 else lane < width + by
        return jnp.where(inside, roll(rows, by), 0.0)

    return A2 * (shifted(1) - shifted(-1)) + B4 * (shifted(2) - shifted(-2))


def coupling_rows(first, last, blocks, width):
    total = blocks * width

    def place(row, k):
        parts = []
        if k:
            parts.append(jnp.zeros((1, k * width), F32))
        parts.append(row)
        if k < blocks - 1:
            parts.append(jnp.zeros((1, (blocks - 1 - k) * width), F32))
        return jnp.concatenate(parts, axis=1)

    stacked = jnp.concatenate(
        [place(last[k], k) for k in range(blocks)] + [place(first[k], k) for k in range(blocks)], axis=0
    )
    applied = stencil_line(stacked)
    g_last = []
    for k in range(blocks):
        row = applied[k : k + 1]
        if k:
            row = row - ALPHA * last[k][:, 0:1] * g_last[k - 1]
        g_last.append(row)
    u_first = [None] * blocks
    for k in range(blocks - 1, -1, -1):
        row = applied[blocks + k : blocks + k + 1]
        if k:
            row = row - ALPHA * first[k][:, 0:1] * g_last[k - 1]
        if k < blocks - 1:
            row = row - ALPHA * first[k][:, width - 1 : width] * u_first[k + 1]
        u_first[k] = row
    return g_last, u_first


def pack_kernel(vel, inv, out, heads, tails, sems):
    blocks, width = inv.shape[0], inv.shape[1]
    line = blocks * width
    copy_heads = pltpu.make_async_copy(inv.at[:, pl.ds(0, 16), :], heads, sems.at[0])
    copy_tails = pltpu.make_async_copy(inv.at[:, pl.ds(width - 16, 16), :], tails, sems.at[1])
    copy_heads.start()
    copy_tails.start()
    comps = vel.shape[0]
    for i in range(out.shape[0]):
        columns = slice(128 * i, 128 * i + 128)
        for c in range(comps):
            out[i, 128 * c : 128 * c + 128, :] = vel[c, 0:128, columns]
            out[i, 384 + 32 * c : 416 + 32 * c, :] = vel[c, 128:160, columns]
    copy_heads.wait()
    copy_tails.wait()
    first = [heads[k, 0:1, :] for k in range(blocks)]
    last = [tails[k, 15:16, :] for k in range(blocks)]
    g_last, u_first = coupling_rows(first, last, blocks, width)
    lane = lanes((1, line))
    zero = jnp.zeros((1, line), F32)

    def unit(at):
        return jnp.where(lane == at, 1.0, 0.0)

    rows = []
    for k in range(blocks):
        lo, hi = width * k, width * (k + 1)
        before, after, tip, end = zero, zero, zero, zero
        if k:
            before = -A2 * unit(lo - 1) - B4 * unit(lo - 2) - ALPHA * g_last[k - 1]
            tip = unit(lo - 1)
        if k < blocks - 1:
            after = A2 * unit(hi) + B4 * unit(hi + 1) - ALPHA * u_first[k + 1]
            end = unit(hi)
        rows += [before, before, tip, end, after, after, zero, zero]
    weights = jnp.concatenate(rows, axis=0)
    high, low = split(weights)
    both = jnp.concatenate([high, low], axis=0)
    pieces = [vel[c, 0:128, :] for c in range(comps)]
    pieces += [vel[c, 128:160, :] for c in range(comps)] + [jnp.zeros((32, line), BF16)]
    count = 8 * blocks
    coded = []
    for piece in (pieces[0], pieces[1], pieces[2], jnp.concatenate(pieces[3:], axis=0)):
        value = lax.dot_general(both, piece, NT, preferred_element_type=F32)
        value = value[0:count] + value[count : 2 * count]
        top = value.astype(BF16).astype(F32)
        place = sublanes(value.shape) % 8
        coded.append(jnp.where((place == 1) | (place == 5), value - top, top))
    for k in range(blocks):
        block = jnp.concatenate([part[8 * k : 8 * k + 8] for part in coded], axis=0).astype(BF16)
        out[2 * k, 480:512, :] = block
        out[2 * k + 1, 480:512, :] = block


def pack(velocity, inverse_x):
    comps, slots, line = velocity.shape
    blocks, width, _ = inverse_x.shape
    return pl.pallas_call(
        pack_kernel,
        out_shape=jax.ShapeDtypeStruct((line // 128, 512, 128), BF16),
        in_specs=[pl.BlockSpec(memory_space=pltpu.VMEM), pl.BlockSpec(memory_space=pl.ANY)],
        out_specs=pl.BlockSpec(memory_space=pltpu.VMEM),
        scratch_shapes=[
            pltpu.VMEM((blocks, 16, width), F32),
            pltpu.VMEM((blocks, 16, width), F32),
            pltpu.SemaphoreType.DMA((2,)),
        ],
        compiler_params=pltpu.CompilerParams(vmem_limit_bytes=24 * MIB),
    )(velocity, inverse_x)


def weights_kernel(where, inv_x, inv_y, metric, out_y, out_x, own, sem):
    blocks, width = inv_y.shape[0], inv_y.shape[1]
    copy = pltpu.make_async_copy(inv_x.at[where[0], pl.ds(where[1] * 128, 128), :], own, sem)
    copy.start()
    first = [inv_y[k, 0:1, :] for k in range(blocks)]
    last = [inv_y[k, width - 1 : width, :] for k in range(blocks)]
    g_last, u_first = coupling_rows(first, last, blocks, width)
    size = blocks * width
    for k in range(blocks):
        for half in range(width // 128):
            here = slice(128 * half, 128 * half + 128)
            tile = inv_y[k, here, :]
            side = jnp.zeros((128, 128), F32)
            local = stencil(jnp.concatenate([side, tile, side], axis=1))
            parts = []
            if k > 1:
                parts.append(jnp.zeros((128, (k - 1) * width + 128), F32))
            elif k:
                parts.append(jnp.zeros((128, 128), F32))
            begin = 0 if k else 128
            end = 512 if k < blocks - 1 else 384
            parts.append(local[:, begin:end])
            rest = size - (k * width + (end - 128))
            if rest:
                parts.append(jnp.zeros((128, rest), F32))
            full = jnp.concatenate(parts, axis=1) if len(parts) > 1 else parts[0]
            if k:
                full = full - tile[:, 0:1] * (ALPHA * g_last[k - 1])
            if k < blocks - 1:
                full = full - tile[:, width - 1 : width] * (ALPHA * u_first[k + 1])
            at = k * width + 128 * half
            scale = jnp.broadcast_to(metric[at // 128 : at // 128 + 1, :], (128, 128)).T
            full = full * jnp.concatenate([scale] * (size // 128), axis=1)
            high, low = split(full)
            out_y[0, at : at + 128, :] = high
            out_y[1, at : at + 128, :] = low
    copy.wait()
    tile = own[...]
    side = jnp.zeros((128, 128), F32)
    local = stencil(jnp.concatenate([side, tile, side], axis=1))
    left, right = local[:, 128:256], local[:, 256:384]
    flip = where[1] == 0
    mine = jnp.where(flip, left, right)
    other = jnp.where(flip, right, left)
    lane = lanes((128, 128))
    parts = [mine, other]
    for c in range(3):
        at = lane - 8 * c
        value = jnp.where((at == 0) | (at == 1), tile[:, 0:1], 0.0)
        value = jnp.where(at == 2, -B4 * tile[:, 1:2], value)
        value = jnp.where(at == 3, B4 * tile[:, width - 2 : width - 1], value)
        value = jnp.where((at == 4) | (at == 5), tile[:, width - 1 : width], value)
        parts.append(value)
    high, low = split(jnp.concatenate(parts, axis=1))
    out_x[0:128, :] = high
    out_x[128:256, :] = low


def build_weights(where, inverse_x, inverse_y, metric):
    blocks, width, _ = inverse_y.shape
    size = blocks * width
    return pl.pallas_call(
        weights_kernel,
        out_shape=(
            jax.ShapeDtypeStruct((2, size, size), BF16),
            jax.ShapeDtypeStruct((256, 640), BF16),
        ),
        in_specs=[
            pl.BlockSpec(memory_space=pltpu.SMEM),
            pl.BlockSpec(memory_space=pl.ANY),
            pl.BlockSpec(memory_space=pltpu.VMEM),
            pl.BlockSpec(memory_space=pltpu.VMEM),
        ],
        out_specs=(pl.BlockSpec(memory_space=pltpu.VMEM), pl.BlockSpec(memory_space=pltpu.VMEM)),
        scratch_shapes=[pltpu.VMEM((128, width), F32), pltpu.SemaphoreType.DMA],
        compiler_params=pltpu.CompilerParams(vmem_limit_bytes=32 * MIB),
        cost_estimate=pl.CostEstimate(flops=20_000_000, bytes_accessed=6_000_000, transcendentals=0),
    )(where, inverse_x, inverse_y, metric)


def compact_kernel(lengths, recv, packed, extras):
    sources = recv.shape[0]
    starts, total = [], jnp.int32(0)
    for s in range(sources):
        starts.append(total)
        total = total + lengths[0, s]
    targets = []
    lane = lanes((1, 256))
    for tile in range(5):
        if tile < 4:
            slot = lane % 128
            source = lane // 128 + 2 * tile
            names = (2 * tile, 2 * tile + 1)
        else:
            slot = 128 + lane % 32
            source = lane // 32
            names = range(sources)
        target = jnp.full((1, 256), -1, jnp.int32)
        for s in names:
            target = jnp.where((source == s) & (slot < lengths[0, s]), starts[s] + slot, target)
        targets.append(target)
    coded = [recv[s, 480:512, :].astype(F32) for s in range(sources)]
    pad = jnp.zeros((104, 256), F32)
    small = lanes((8, 128)) // 32
    data, feats = [], []
    for tile in range(5):
        columns = []
        for c in range(3):
            if tile < 4:
                block = recv[2 * tile : 2 * tile + 2, 128 * c : 128 * c + 128, :]
            else:
                block = recv[:, 384 + 32 * c : 416 + 32 * c, :]
            columns.append(block.reshape(256, 128))
        data.append(jnp.concatenate(columns, axis=1))
        if tile < 4:
            block = jnp.concatenate([coded[2 * tile][0:24], coded[2 * tile + 1][0:24]], axis=1)
        else:
            halves = []
            for first in (0, 4):
                rows = []
                for c in range(3):
                    value = jnp.zeros((8, 128), F32)
                    for q in range(4):
                        value = jnp.where(small == q, roll(coded[first + q][24:32], 32 * (q - c)), value)
                    rows.append(value)
                halves.append(jnp.concatenate(rows, axis=0))
            block = jnp.concatenate(halves, axis=1)
        feats.append(jnp.concatenate([block, pad], axis=0).astype(BF16))
    for part in range(4):
        row = sublanes((256, 256)) + 256 * part
        sums = jnp.zeros((256, 384), F32)
        coupled = jnp.zeros((256, 128), F32)
        for tile in range(5):
            pick = jnp.where(row == targets[tile], 1.0, 0.0).astype(BF16)
            sums = sums + jnp.dot(pick, data[tile], preferred_element_type=F32)
            coupled = coupled + lax.dot_general(pick, feats[tile], NT, preferred_element_type=F32)
        packed[256 * part : 256 * part + 256, :] = sums.astype(BF16)
        extras[256 * part : 256 * part + 256, :] = coupled.astype(BF16)


def compact(lengths, recv):
    return pl.pallas_call(
        compact_kernel,
        out_shape=(jax.ShapeDtypeStruct((1024, 384), BF16), jax.ShapeDtypeStruct((1024, 128), BF16)),
        in_specs=[pl.BlockSpec(memory_space=pltpu.SMEM), pl.BlockSpec(memory_space=pltpu.VMEM)],
        out_specs=(pl.BlockSpec(memory_space=pltpu.VMEM), pl.BlockSpec(memory_space=pltpu.VMEM)),
        compiler_params=pltpu.CompilerParams(vmem_limit_bytes=24 * MIB),
    )(lengths, recv)


def normal_kernel(packed, weights, out, held, sem):
    field = packed[...]
    for part in range(4):
        here = slice(256 * part, 256 * part + 256)
        value = jnp.dot(weights[0, here, :], field, preferred_element_type=F32)
        value = value + jnp.dot(weights[1, here, :], field, preferred_element_type=F32)
        for c in range(3):
            held[16 * part : 16 * part + 16, 16 * c : 16 * c + 16, :] = (
                value[:, 128 * c : 128 * c + 128].astype(BF16).reshape(16, 16, 128)
            )
    copy = pltpu.make_async_copy(held, out.at[:, pl.ds(48, 48), :], sem)
    copy.start()
    copy.wait()


def normal(packed, weights):
    return pl.pallas_call(
        normal_kernel,
        out_shape=jax.ShapeDtypeStruct((64, 96, 128), BF16),
        in_specs=[pl.BlockSpec(memory_space=pltpu.VMEM), pl.BlockSpec(memory_space=pltpu.VMEM)],
        out_specs=pl.BlockSpec(memory_space=pl.ANY),
        scratch_shapes=[pltpu.VMEM((64, 48, 128), BF16), pltpu.SemaphoreType.DMA],
        compiler_params=pltpu.CompilerParams(vmem_limit_bytes=24 * MIB),
        cost_estimate=pl.CostEstimate(flops=1_600_000_000, bytes_accessed=6_000_000, transcendentals=0),
    )(packed, weights)


def stream_kernel(packed, partner, extras, weights, sent, out, held, sem):
    del sent
    coupled = extras[...]
    for c in range(3):
        columns = slice(128 * c, 128 * c + 128)
        field = jnp.concatenate([packed[:, columns], partner[:, columns]], axis=1)
        value = lax.dot_general(field, weights[:, 0:256], NT, preferred_element_type=F32)
        value = value + lax.dot_general(
            coupled, weights[:, 256 + 128 * c : 384 + 128 * c], NT, preferred_element_type=F32
        )
        value = value[:, 0:128] + value[:, 128:256]
        held[:, 16 * c : 16 * c + 16, :] = value.astype(BF16).reshape(64, 16, 128)
    copy = pltpu.make_async_copy(held, out.at[:, pl.ds(0, 48), :], sem)
    copy.start()
    copy.wait()


def stream(packed, partner, extras, weights, sent):
    vmem = pl.BlockSpec(memory_space=pltpu.VMEM)
    return pl.pallas_call(
        stream_kernel,
        out_shape=jax.ShapeDtypeStruct((64, 96, 128), BF16),
        in_specs=[vmem, vmem, vmem, vmem, pl.BlockSpec(memory_space=pl.ANY)],
        out_specs=pl.BlockSpec(memory_space=pl.ANY),
        scratch_shapes=[pltpu.VMEM((64, 48, 128), BF16), pltpu.SemaphoreType.DMA],
        input_output_aliases={4: 0},
        compiler_params=pltpu.CompilerParams(vmem_limit_bytes=24 * MIB),
    )(packed, partner, extras, weights, sent)


def unpack_kernel(recv, out_x, out_y, sems):
    copies = []
    for which, out in enumerate((out_x, out_y)):
        for c in range(3):
            copies.append(
                pltpu.make_async_copy(
                    recv.at[:, pl.ds(48 * which + 16 * c, 16), :], out.at[c], sems.at[3 * which + c]
                )
            )
    for copy in copies:
        copy.start()
    for copy in copies:
        copy.wait()


def unpack(recv):
    shape = jax.ShapeDtypeStruct((3, 64, 16, 128), BF16)
    anywhere = pl.BlockSpec(memory_space=pl.ANY)
    return pl.pallas_call(
        unpack_kernel,
        out_shape=(shape, shape),
        in_specs=[anywhere],
        out_specs=(anywhere, anywhere),
        scratch_shapes=[pltpu.SemaphoreType.DMA((6,))],
        compiler_params=pltpu.CompilerParams(vmem_limit_bytes=16 * MIB),
    )(recv)


def local(velocity, lengths, inverse_x, inverse_y, metric):
    rank = lax.axis_index("row")
    where = jnp.stack([rank // 2, rank % 2]).astype(jnp.int32)
    sent = pack(velocity[:, 0], inverse_x)
    weights_y, weights_x = build_weights(where, inverse_x, inverse_y, metric.reshape(8, 128))
    received = lax.all_to_all(sent, "row", split_axis=0, concat_axis=0, tiled=True)
    packed, extras = compact(lengths, received)
    partner = lax.ppermute(packed, "row", [(i, i ^ 1) for i in range(8)])
    result = normal(packed, weights_y)
    result = stream(packed, partner, extras, weights_x, result)
    moved = lax.all_to_all(result, "col", split_axis=0, concat_axis=0, tiled=True)
    return unpack(moved)


def solution(mesh):
    return jax.shard_map(
        local,
        mesh=mesh,
        in_specs=(P(None, "col", "row", None), P("col", None), P(), P(), P()),
        out_specs=(P(None, None, "col", "row"), P(None, None, "col", "row")),
        check_vma=False,
    )
```

time: 182 us -> 109 us (0.60)
  blocking collectives: 0 us -> 90.2 us
  waiting for transfers between devices: 64.3 us -> 0.01 us
  local copies, waits for them, and re-layouts: 57.1 us -> 2.44 us
  starting transfers between devices: 38.9 us -> 2.65 us
  Pallas kernels: 0 us -> 12.9 us
  other arithmetic: 12.9 us -> 0.08 us
  matrix products: 6.58 us -> 0 us
    all_to_all x0 -> x2, blocking collectives: none -> 90.2 us  [the longest x1 53.4 us: local(): lax.all_to_all(result, 'col', split_axis=0, concat_axis=0, tiled=True)]
    all_to_all x4 -> x0, waiting for transfers between devices: 64.3 us -> none  [the longest x1 26 us: local(): lax.all_to_all(derived_y, 'col', split_axis=2, concat_axis=1, tiled=True)]
    all_to_all x4 -> x0, starting transfers between devices: 38.9 us -> none  [the longest x1 15.1 us: local(): lax.all_to_all(packed_slopes, 'col', split_axis=2, concat_axis=1, tiled=T...]
    all_to_all x5 -> x0, local copies, waits for them, and re-layouts: 18.3 us -> none  [the longest x2 9.91 us: local(): lax.all_to_all(derived_x, 'row', split_axis=3, concat_axis=2, tiled=True)]
    unnamed x20 -> x12, local copies, waits for them, and re-layouts: 19.9 us -> 2.44 us
    gather x4 -> x0, local copies, waits for them, and re-layouts: 13.4 us -> none  [take_plane(): return jnp.take(values, sources, axis=1)]
    pallas_call x0 -> x6, Pallas kernels: none -> 12.9 us  [the longest x1 3.52 us: build_weights(): pl.pallas_call(weights_kernel, out_shape=(jax.ShapeDtypeStruct((2, size,...]
    dot_general x8 -> x0, matrix products: 6.58 us -> none  [the longest x4 4.19 us: apply_block(): jnp.einsum('ij,cajx->caix', inverse, block_now, precision=lax.Precision.H...]
  transfers between devices with their start and end apart: 4 -> 1, of which waited for: 4 -> 0; matrix products, arithmetic and copies ran while one was open for 21% -> 0% of each run, Pallas kernels for 0% -> 5%
where the time goes in v1:
time: 109 us
  blocking collectives  90.2 us (83%)
  Pallas kernels  12.9 us (12%)
  starting transfers between devices  2.65 us (2%)
  local copies, waits for them, and re-layouts  2.44 us (2%)
    all_to_all x1, blocking collectives, local(): lax.all_to_all(result, 'col', split_axis=0, concat_axis=0, tiled=True)  53.4 us
    all_to_all x1, blocking collectives, local(): lax.all_to_all(sent, 'row', split_axis=0, concat_axis=0, tiled=True)  36.8 us
    pallas_call x1, Pallas kernels, build_weights(): pl.pallas_call(weights_kernel, out_shape=(jax.ShapeDtypeStruct((2, size,...  3.52 us
    pallas_call x1, Pallas kernels, compact(): pl.pallas_call(compact_kernel, out_shape=(jax.ShapeDtypeStruct((1024, 384...  2.77 us
    ppermute x1, starting transfers between devices, local(): partner = lax.ppermute(packed, 'row', [(i, i ^ 1) for i in range(8)])  2.65 us
    pallas_call x1, Pallas kernels, normal(): pl.pallas_call(normal_kernel, out_shape=jax.ShapeDtypeStruct((64, 96, 128...  2.46 us
    unnamed x12, local copies, waits for them, and re-layouts  2.44 us
    pallas_call x1, Pallas kernels, stream(): pl.pallas_call(stream_kernel, out_shape=jax.ShapeDtypeStruct((64, 96, 128...  2.19 us
  transfers between devices with their start and end apart: 1, of which 0 were waited for; matrix products, arithmetic and copies ran while one was open for 0% of the time, Pallas kernels for 5%

profile of v1, /device:TPU:1, one launch (start us, length us, event | category | flops | bytes accessed | tf_op | source)
XLA Modules:
  0.0 109.0 jit_solution(12937787138418545546)
XLA Ops:
  0.6 0.0 copy-start
  0.6 1.2 %copy-done = f32[4,256,256]{2,1,0:T(8,128)S(1)} copy-done((f32[4,256,256]{2,1,0:T(8,128)S(1)}, f32[4,256,256]{2,1,0:T(8,128)}, u32[]{:S(2)}) %copy-start) | copy-done | bytes 1048600
  1.9 0.0 copy-start.3
  1.9 1.2 %copy-done.3 = bf16[3,1,160,1024]{3,2,1,0:T(8,128)(2,1)S(1)} copy-done((bf16[3,1,160,1024]{3,2,1,0:T(8,128)(2,1)S(1)}, bf16[3,1,160,1024]{3,2,1,0:T(8,128)(2,1)}, u32[]{:S(2)}) %copy-start.3) | copy-done | bytes 983064
  3.1 0.0 copy-start.5
  3.1 0.8 shard_map.68
  3.9 0.0 copy-start.1
  3.9 0.0 copy-start.2
  3.9 0.0 copy-start.4
  3.9 36.8 %all_to_all.10.recv = bf16[8,512,128]{2,1,0:T(8,128)(2,1)S(1)} all-to-all(bf16[8,512,128]{2,1,0:T(8,128)(2,1)S(1)} %shard_map.68), channel_id=1, replica_groups=mesh['row'=8,'col'=64] {'row'}, dimensions={0} | all-to-all | bytes 2097152 | tf_op jit(solution)/shard_map/all_to_all | solution.py:393
  40.7 0.0 copy-done.5
  40.7 2.8 %shard_map.69 = (bf16[1024,384]{1,0:T(8,128)(2,1)S(1)}, bf16[1024,128]{1,0:T(8,128)(2,1)S(1)}) custom-call(s32[1,8]{1,0:T(1,128)S(1)} %copy-done.5, bf16[8,512,128]{2,1,0:T(8,128)(2,1)S(1)} %all_to_all.10.recv), custom_call_target="tpu_custom_call" | custom-call | tf_op jit(solution)/shard_map/pallas_call | solution.py:294
  43.5 2.6 %collective-permute-start = (bf16[1024,384]{1,0:T(8,128)(2,1)S(1)}, bf16[1024,384]{1,0:T(8,128)(2,1)}, u32[]{:S(2)}, u32[]{:S(2)}) collective-permute-start(bf16[1024,384]{1,0:T(8,128)(2,1)S(1)} %get-tuple-element.6.packed), channel_id=1, source_target_pairs={{0,64},{64,0},{128,192},{192,128},{256,320},{320,256},{384,448},{4... | collective-permute-start | bytes 2359304 | tf_op jit(solution)/shard_map/ppermute | solution.py:395
  46.2 0.1 pad_add_fusion.where
  46.3 0.0 copy-done.1
  46.3 0.0 copy-done.2
  46.3 0.0 copy-done.4
  46.3 3.5 %shard_map.70 = (bf16[2,1024,1024]{2,1,0:T(8,128)(2,1)S(1)}, bf16[256,640]{1,0:T(8,128)(2,1)S(1)}) custom-call(s32[2]{0:T(128)S(1)} %pad_add_fusion.where, f32[4,256,256]{2,1,0:T(8,128)S(1)} %copy-done.1, f32[4,256,256]{2,1,0:T(8,128)S(1)} %copy-done.2, f32[8,128]{1,0:T(8,128)S(1)} %bitcast.5), custom_call_target="tpu_custom_call" | custom-call | flops 20000000 | bytes 6000000 | tf_op jit(solution)/shard_map/pallas_call | solution.py:214
  49.8 2.5 %shard_map.71.sent = bf16[64,96,128]{2,1,0:T(8,128)(2,1)S(1)} custom-call(bf16[1024,384]{1,0:T(8,128)(2,1)S(1)} %get-tuple-element.6.packed, bf16[2,1024,1024]{2,1,0:T(8,128)(2,1)S(1)} %get-tuple-element.9.weights), custom_call_target="tpu_custom_call" | custom-call | flops 1600000000 | bytes 6000000 | tf_op jit(solution)/shard_map/pallas_call | solution.py:319
  52.3 0.0 collective-permute-done.partner
  52.3 2.2 %shard_map.72 = bf16[64,96,128]{2,1,0:T(8,128)(2,1)S(1)} custom-call(bf16[1024,384]{1,0:T(8,128)(2,1)S(1)} %get-tuple-element.6.packed, bf16[1024,384]{1,0:T(8,128)(2,1)} %collective-permute-done.partner, bf16[1024,128]{1,0:T(8,128)(2,1)S(1)} %get-tuple-element.7.extras, ...), custom_call_target="tpu_custom_call", output_to_operand_aliasing={{}: (4, {})} | custom-call | tf_op jit(solution)/shard_map/pallas_call | solution.py:349
  54.5 53.4 %all_to_all.11.recv = bf16[64,96,128]{2,1,0:T(8,128)(2,1)S(1)} all-to-all(bf16[64,96,128]{2,1,0:T(8,128)(2,1)S(1)} %shard_map.72), channel_id=1, replica_groups=mesh['row'=8,'col'=64] {'col'}, dimensions={0} | all-to-all | bytes 3145728 | tf_op jit(solution)/shard_map/all_to_all | solution.py:398
  107.8 1.2 %shard_map.73 = (bf16[3,64,16,128]{3,2,1,0:T(8,128)(2,1)}, bf16[3,64,16,128]{3,2,1,0:T(8,128)(2,1)}) custom-call(bf16[64,96,128]{2,1,0:T(8,128)(2,1)S(1)} %all_to_all.11.recv), custom_call_target="tpu_custom_call" | custom-call | tf_op jit(solution)/shard_map/pallas_call | solution.py:378
Async XLA Ops:
  0.6 1.2 %copy-start = (f32[4,256,256]{2,1,0:T(8,128)S(1)}, f32[4,256,256]{2,1,0:T(8,128)}, u32[]{:S(2)}) copy-start(f32[4,256,256]{2,1,0:T(8,128)} %inv_x.1) | copy-start | bytes 3145732
  1.9 1.2 %copy-start.3 = (bf16[3,1,160,1024]{3,2,1,0:T(8,128)(2,1)S(1)}, bf16[3,1,160,1024]{3,2,1,0:T(8,128)(2,1)}, u32[]{:S(2)}) copy-start(bf16[3,1,160,1024]{3,2,1,0:T(8,128)(2,1)} %param.5) | copy-start | bytes 2949124
  3.1 37.7 %copy-start.5 = (s32[1,8]{1,0:T(1,128)S(1)}, s32[1,8]{1,0:T(1,128)}, u32[]{:S(2)}) copy-start(s32[1,8]{1,0:T(1,128)} %lengths.1) | copy-start | bytes 100
  3.9 42.4 %copy-start.1 = (f32[4,256,256]{2,1,0:T(8,128)S(1)}, f32[4,256,256]{2,1,0:T(8,128)}, u32[]{:S(2)}) copy-start(f32[4,256,256]{2,1,0:T(8,128)} %inv_x.1) | copy-start | bytes 3145732
  3.9 42.4 %copy-start.2 = (f32[4,256,256]{2,1,0:T(8,128)S(1)}, f32[4,256,256]{2,1,0:T(8,128)}, u32[]{:S(2)}) copy-start(f32[4,256,256]{2,1,0:T(8,128)} %inv_y.1) | copy-start | bytes 3145732
  3.9 42.4 %copy-start.4 = (f32[1024]{0:T(1024)S(1)}, f32[1024]{0:T(1024)}, u32[]{:S(2)}) copy-start(f32[1024]{0:T(1024)} %param.9) | copy-start | bytes 12292
  43.5 8.8 %collective-permute-start = (bf16[1024,384]{1,0:T(8,128)(2,1)S(1)}, bf16[1024,384]{1,0:T(8,128)(2,1)}, u32[]{:S(2)}, u32[]{:S(2)}) collective-permute-start(bf16[1024,384]{1,0:T(8,128)(2,1)S(1)} %get-tuple-element.6.packed), channel_id=1, source_target_pairs={{0,64},{64,0},{128,192},{192,128},{256,320},{320,256},{384,448},{4... | collective-permute-start | bytes 2359304 | tf_op jit(solution)/shard_map/ppermute | solution.py:395

commit v2 on v1

--- a/solution.py
+++ b/solution.py
@@ -12,6 +12,10 @@
 BF16 = jnp.bfloat16
 NT = (((1,), (1,)), ((), ()))
 MIB = 1 << 20
+fixed = pltpu.with_memory_space_constraint
+ROW = (4, 5, 0, 1, 6, 7, 2, 3)
+COL = (7, 6, 5, 4, 3, 2, 1, 0)
+SPANS = ((0, 48), (48, 48), (96, 64))
 
 
 def lanes(shape):
@@ -79,7 +83,7 @@
     return g_last, u_first
 
 
-def pack_kernel(vel, inv, out, heads, tails, sems):
+def pack_kernel(vel_hbm, inv, out, vel, heads, tails, sems):
     blocks, width = inv.shape[0], inv.shape[1]
     line = blocks * width
     copy_heads = pltpu.make_async_copy(inv.at[:, pl.ds(0, 16), :], heads, sems.at[0])
@@ -87,11 +91,13 @@
     copy_heads.start()
     copy_tails.start()
     comps = vel.shape[0]
-    for i in range(out.shape[0]):
-        columns = slice(128 * i, 128 * i + 128)
-        for c in range(comps):
-            out[i, 128 * c : 128 * c + 128, :] = vel[c, 0:128, columns]
-            out[i, 384 + 32 * c : 416 + 32 * c, :] = vel[c, 128:160, columns]
+    copies = []
+    for c in range(comps):
+        for number, (begin, size) in enumerate(SPANS):
+            here = (c, pl.ds(begin, size))
+            copy = pltpu.make_async_copy(vel_hbm.at[here], vel.at[here], sems.at[2 + len(SPANS) * c + number])
+            copy.start()
+            copies.append(copy)
     copy_heads.wait()
     copy_tails.wait()
     first = [heads[k, 0:1, :] for k in range(blocks)]
@@ -117,6 +123,13 @@
     weights = jnp.concatenate(rows, axis=0)
     high, low = split(weights)
     both = jnp.concatenate([high, low], axis=0)
+    for copy in copies:
+        copy.wait()
+    for i in range(out.shape[0]):
+        columns = slice(128 * ROW[i], 128 * ROW[i] + 128)
+        for c in range(comps):
+            out[i, 128 * c : 128 * c + 128, :] = vel[c, 0:128, columns]
+            out[i, 384 + 32 * c : 416 + 32 * c, :] = vel[c, 128:160, columns]
     pieces = [vel[c, 0:128, :] for c in range(comps)]
     pieces += [vel[c, 128:160, :] for c in range(comps)] + [jnp.zeros((32, line), BF16)]
     count = 8 * blocks
@@ -129,8 +142,8 @@
         coded.append(jnp.where((place == 1) | (place == 5), value - top, top))
     for k in range(blocks):
         block = jnp.concatenate([part[8 * k : 8 * k + 8] for part in coded], axis=0).astype(BF16)
-        out[2 * k, 480:512, :] = block
-        out[2 * k + 1, 480:512, :] = block
+        out[ROW.index(2 * k), 480:512, :] = block
+        out[ROW.index(2 * k + 1), 480:512, :] = block
 
 
 def pack(velocity, inverse_x):
@@ -139,15 +152,16 @@
     return pl.pallas_call(
         pack_kernel,
         out_shape=jax.ShapeDtypeStruct((line // 128, 512, 128), BF16),
-        in_specs=[pl.BlockSpec(memory_space=pltpu.VMEM), pl.BlockSpec(memory_space=pl.ANY)],
+        in_specs=[pl.BlockSpec(memory_space=pltpu.HBM), pl.BlockSpec(memory_space=pltpu.HBM)],
         out_specs=pl.BlockSpec(memory_space=pltpu.VMEM),
         scratch_shapes=[
+            pltpu.VMEM(velocity.shape, BF16),
             pltpu.VMEM((blocks, 16, width), F32),
             pltpu.VMEM((blocks, 16, width), F32),
-            pltpu.SemaphoreType.DMA((2,)),
+            pltpu.SemaphoreType.DMA((2 + len(SPANS) * comps,)),
         ],
         compiler_params=pltpu.CompilerParams(vmem_limit_bytes=24 * MIB),
-    )(velocity, inverse_x)
+    )(fixed(velocity, pltpu.HBM), fixed(inverse_x, pltpu.HBM))
 
 
 def weights_kernel(where, inv_x, inv_y, metric, out_y, out_x, own, sem):
@@ -249,7 +263,8 @@
             names = range(sources)
         target = jnp.full((1, 256), -1, jnp.int32)
         for s in names:
-            target = jnp.where((source == s) & (slot < lengths[0, s]), starts[s] + slot, target)
+            held = (source == s) & (slot < lengths[0, ROW[s]])
+            target = jnp.where(held, starts[ROW[s]] + slot, target)
         targets.append(target)
     coded = [recv[s, 480:512, :].astype(F32) for s in range(sources)]
     pad = jnp.zeros((104, 256), F32)
@@ -300,35 +315,54 @@
     )(lengths, recv)
 
 
-def normal_kernel(packed, weights, out, held, sem):
+def normal_kernel(packed, weights_hbm, out, held, weights, sems, loads):
     field = packed[...]
+    copies, fetches = [], []
+    for part in range(4):
+        here = (slice(None), pl.ds(256 * part, 256))
+        fetches.append(pltpu.make_async_copy(weights_hbm.at[here], weights.at[here], loads.at[part]))
+        fetches[-1].start()
     for part in range(4):
         here = slice(256 * part, 256 * part + 256)
+        fetches[part].wait()
         value = jnp.dot(weights[0, here, :], field, preferred_element_type=F32)
         value = value + jnp.dot(weights[1, here, :], field, preferred_element_type=F32)
         for c in range(3):
-            held[16 * part : 16 * part + 16, 16 * c : 16 * c + 16, :] = (
-                value[:, 128 * c : 128 * c + 128].astype(BF16).reshape(16, 16, 128)
+            block = value[:, 128 * c : 128 * c + 128].astype(BF16).reshape(16, 16, 128)
+            for half in range(2):
+                at = 8 * COL.index(2 * part + half)
+                held[at : at + 8, 16 * c : 16 * c + 16, :] = block[8 * half : 8 * half + 8]
+        for half in range(2):
+            rows = pl.ds(8 * COL.index(2 * part + half), 8)
+            copy = pltpu.make_async_copy(
+                held.at[rows], out.at[rows, pl.ds(48, 48), :], sems.at[2 * part + half]
             )
-    copy = pltpu.make_async_copy(held, out.at[:, pl.ds(48, 48), :], sem)
-    copy.start()
-    copy.wait()
+            copy.start()
+            copies.append(copy)
+    for copy in copies:
+        copy.wait()
 
 
 def normal(packed, weights):
     return pl.pallas_call(
         normal_kernel,
         out_shape=jax.ShapeDtypeStruct((64, 96, 128), BF16),
-        in_specs=[pl.BlockSpec(memory_space=pltpu.VMEM), pl.BlockSpec(memory_space=pltpu.VMEM)],
+        in_specs=[pl.BlockSpec(memory_space=pltpu.VMEM), pl.BlockSpec(memory_space=pltpu.HBM)],
         out_specs=pl.BlockSpec(memory_space=pl.ANY),
-        scratch_shapes=[pltpu.VMEM((64, 48, 128), BF16), pltpu.SemaphoreType.DMA],
+        scratch_shapes=[
+            pltpu.VMEM((64, 48, 128), BF16),
+            pltpu.VMEM(weights.shape, BF16),
+            pltpu.SemaphoreType.DMA((8,)),
+            pltpu.SemaphoreType.DMA((4,)),
+        ],
         compiler_params=pltpu.CompilerParams(vmem_limit_bytes=24 * MIB),
         cost_estimate=pl.CostEstimate(flops=1_600_000_000, bytes_accessed=6_000_000, transcendentals=0),
-    )(packed, weights)
-
-
-def stream_kernel(packed, partner, extras, weights, sent, out, held, sem):
+    )(packed, fixed(weights, pltpu.HBM))
+
+
+def stream_kernel(packed, partner, extras, weights, sent, out, held, sems):
     del sent
+    copies = []
     coupled = extras[...]
     for c in range(3):
         columns = slice(128 * c, 128 * c + 128)
@@ -338,10 +372,16 @@
             coupled, weights[:, 256 + 128 * c : 384 + 128 * c], NT, preferred_element_type=F32
         )
         value = value[:, 0:128] + value[:, 128:256]
-        held[:, 16 * c : 16 * c + 16, :] = value.astype(BF16).reshape(64, 16, 128)
-    copy = pltpu.make_async_copy(held, out.at[:, pl.ds(0, 48), :], sem)
-    copy.start()
-    copy.wait()
+        rows = pl.ds(16 * c, 16)
+        block = value.astype(BF16).reshape(64, 16, 128)
+        for run in range(8):
+            at = 8 * COL.index(run)
+            held[at : at + 8, 16 * c : 16 * c + 16, :] = block[8 * run : 8 * run + 8]
+        copy = pltpu.make_async_copy(held.at[:, rows, :], out.at[:, rows, :], sems.at[c])
+        copy.start()
+        copies.append(copy)
+    for copy in copies:
+        copy.wait()
 
 
 def stream(packed, partner, extras, weights, sent):
@@ -351,7 +391,7 @@
         out_shape=jax.ShapeDtypeStruct((64, 96, 128), BF16),
         in_specs=[vmem, vmem, vmem, vmem, pl.BlockSpec(memory_space=pl.ANY)],
         out_specs=pl.BlockSpec(memory_space=pl.ANY),
-        scratch_shapes=[pltpu.VMEM((64, 48, 128), BF16), pltpu.SemaphoreType.DMA],
+        scratch_shapes=[pltpu.VMEM((64, 48, 128), BF16), pltpu.SemaphoreType.DMA((4,))],
         input_output_aliases={4: 0},
         compiler_params=pltpu.CompilerParams(vmem_limit_bytes=24 * MIB),
     )(packed, partner, extras, weights, sent)
@@ -361,11 +401,14 @@
     copies = []
     for which, out in enumerate((out_x, out_y)):
         for c in range(3):
-            copies.append(
-                pltpu.make_async_copy(
-                    recv.at[:, pl.ds(48 * which + 16 * c, 16), :], out.at[c], sems.at[3 * which + c]
+            for run in range(8):
+                copies.append(
+                    pltpu.make_async_copy(
+                        recv.at[pl.ds(8 * COL.index(run), 8), pl.ds(48 * which + 16 * c, 16), :],
+                        out.at[c, pl.ds(8 * run, 8)],
+                        sems.at[3 * which + c, run],
+                    )
                 )
-            )
     for copy in copies:
         copy.start()
     for copy in copies:
@@ -380,22 +423,32 @@
         out_shape=(shape, shape),
         in_specs=[anywhere],
         out_specs=(anywhere, anywhere),
-        scratch_shapes=[pltpu.SemaphoreType.DMA((6,))],
+        scratch_shapes=[pltpu.SemaphoreType.DMA((6, 8))],
         compiler_params=pltpu.CompilerParams(vmem_limit_bytes=16 * MIB),
     )(recv)
 
 
 def local(velocity, lengths, inverse_x, inverse_y, metric):
     rank = lax.axis_index("row")
-    where = jnp.stack([rank // 2, rank % 2]).astype(jnp.int32)
+    where = jnp.stack([lax.shift_right_logical(rank, 1), rank & 1]).astype(jnp.int32)
     sent = pack(velocity[:, 0], inverse_x)
-    weights_y, weights_x = build_weights(where, inverse_x, inverse_y, metric.reshape(8, 128))
-    received = lax.all_to_all(sent, "row", split_axis=0, concat_axis=0, tiled=True)
+    weights = build_weights(where, inverse_x, inverse_y, metric.reshape(8, 128))
+    received = lax.all_to_all(
+        sent, "row", split_axis=0, concat_axis=0, tiled=True, axis_index_groups=[list(ROW)]
+    )
+    received, (weights_y, weights_x) = lax.optimization_barrier((received, weights))
     packed, extras = compact(lengths, received)
     partner = lax.ppermute(packed, "row", [(i, i ^ 1) for i in range(8)])
     result = normal(packed, weights_y)
     result = stream(packed, partner, extras, weights_x, result)
-    moved = lax.all_to_all(result, "col", split_axis=0, concat_axis=0, tiled=True)
+    moved = lax.all_to_all(
+        result,
+        "col",
+        split_axis=0,
+        concat_axis=0,
+        tiled=True,
+        axis_index_groups=[[8 * run + i for run in COL for i in range(8)]],
+    )
     return unpack(moved)
 
 

time: 109 us -> 102 us (0.936)
  blocking collectives: 90.2 us -> 50.1 us
  waiting for transfers between devices: 0.01 us -> 15.4 us
  starting transfers between devices: 2.65 us -> 16.3 us
  Pallas kernels: 12.9 us -> 17 us
    all_to_all x2 -> x1, blocking collectives: 90.2 us -> 50.1 us  [local(): lax.all_to_all(result, 'col', split_axis=0, concat_axis=0, tiled=True, ax...]
    all_to_all x0 -> x1, waiting for transfers between devices: none -> 15.4 us  [local(): lax.all_to_all(sent, 'row', split_axis=0, concat_axis=0, tiled=True, axis...]
    all_to_all x0 -> x1, starting transfers between devices: none -> 13.9 us  [local(): lax.all_to_all(sent, 'row', split_axis=0, concat_axis=0, tiled=True, axis...]
    pallas_call x1, Pallas kernels: 0.81 us -> 2.86 us  [pack(): pl.pallas_call(pack_kernel, out_shape=jax.ShapeDtypeStruct((line // 128,...]
    pallas_call x1, Pallas kernels: 2.46 us -> 4.38 us  [normal(): pl.pallas_call(normal_kernel, out_shape=jax.ShapeDtypeStruct((64, 96, 128...]
    unnamed x12 -> x10, local copies, waits for them, and re-layouts: 2.44 us -> 1.96 us
  transfers between devices with their start and end apart: 1 -> 2, of which waited for: 0 -> 1; matrix products, arithmetic and copies ran while one was open for 0% -> 0% of each run, Pallas kernels for 5% -> 8%
where the time goes in v2:
time: 102 us
  blocking collectives  50.1 us (49%)
  Pallas kernels  17 us (17%)
  starting transfers between devices  16.3 us (16%)
  waiting for transfers between devices  15.4 us (15%)
  local copies, waits for them, and re-layouts  1.96 us (2%)
    all_to_all x1, blocking collectives, local(): lax.all_to_all(result, 'col', split_axis=0, concat_axis=0, tiled=True, ax...  50.1 us
    all_to_all x1, waiting for transfers between devices, local(): lax.all_to_all(sent, 'row', split_axis=0, concat_axis=0, tiled=True, axis...  15.4 us
    all_to_all x1, starting transfers between devices, local(): lax.all_to_all(sent, 'row', split_axis=0, concat_axis=0, tiled=True, axis...  13.9 us
    pallas_call x1, Pallas kernels, normal(): pl.pallas_call(normal_kernel, out_shape=jax.ShapeDtypeStruct((64, 96, 128...  4.38 us
    pallas_call x1, Pallas kernels, build_weights(): pl.pallas_call(weights_kernel, out_shape=(jax.ShapeDtypeStruct((2, size,...  3.52 us
    pallas_call x1, Pallas kernels, pack(): pl.pallas_call(pack_kernel, out_shape=jax.ShapeDtypeStruct((line // 128,...  2.86 us
    pallas_call x1, Pallas kernels, compact(): pl.pallas_call(compact_kernel, out_shape=(jax.ShapeDtypeStruct((1024, 384...  2.76 us
    ppermute x1, starting transfers between devices, local(): partner = lax.ppermute(packed, 'row', [(i, i ^ 1) for i in range(8)])  2.41 us
  transfers between devices with their start and end apart: 2, of which 1 were waited for; matrix products, arithmetic and copies ran while one was open for 0% of the time, Pallas kernels for 8%

profile of v2, /device:TPU:1, one launch (start us, length us, event | category | flops | bytes accessed | tf_op | source)
XLA Modules:
  0.0 101.6 jit_solution(1711920705422299391)
XLA Ops:
  0.6 2.9 %shard_map.68 = bf16[8,512,128]{2,1,0:T(8,128)(2,1)} custom-call(bf16[3,160,1024]{2,1,0:T(8,128)(2,1)} %bitcast.5, f32[4,256,256]{2,1,0:T(8,128)} %inv_x.1), custom_call_target="tpu_custom_call" | custom-call | tf_op jit(solution)/shard_map/pallas_call | solution.py:152
  3.5 0.0 copy-start
  3.5 0.0 copy-start.2
  3.5 0.0 copy-start.3
  3.5 13.9 %all-to-all-start = ((bf16[8,512,128]{2,1,0:T(8,128)(2,1)}), bf16[8,512,128]{2,1,0:T(8,128)(2,1)S(1)}, u32[]{:S(2)}, u32[]{:S(2)}) async-start(bf16[8,512,128]{2,1,0:T(8,128)(2,1)} %shard_map.68), calls=%async_computation | async-start | bytes 2097152 | tf_op jit(solution)/shard_map/all_to_all | solution.py:436
  17.4 0.0 copy-start.4
  17.4 0.1 pad_add_fusion.where
  17.5 0.0 copy-done
  17.5 0.0 copy-done.2
  17.5 0.0 copy-done.3
  17.5 3.5 %shard_map.69 = (bf16[2,1024,1024]{2,1,0:T(8,128)(2,1)S(1)}, bf16[256,640]{1,0:T(8,128)(2,1)S(1)}) custom-call(s32[2]{0:T(128)S(1)} %pad_add_fusion.where, f32[4,256,256]{2,1,0:T(8,128)S(1)} %copy-done, f32[4,256,256]{2,1,0:T(8,128)S(1)} %copy-done.2, f32[8,128]{1,0:T(8,128)S(1)} %bitcast.4), custom_call_target="tpu_custom_call" | custom-call | flops 20000000 | bytes 6000000 | tf_op jit(solution)/shard_map/pallas_call | solution.py:228
  21.0 0.0 copy-start.1
  21.0 1.9 %copy-done.1 = bf16[2,1024,1024]{2,1,0:T(8,128)(2,1)} copy-done((bf16[2,1024,1024]{2,1,0:T(8,128)(2,1)}, bf16[2,1024,1024]{2,1,0:T(8,128)(2,1)S(1)}, u32[]{:S(2)}) %copy-start.1) | copy-done | bytes 4194328
  23.0 15.4 %all-to-all-done.recv = bf16[8,512,128]{2,1,0:T(8,128)(2,1)S(1)} async-done(((bf16[8,512,128]{2,1,0:T(8,128)(2,1)}), bf16[8,512,128]{2,1,0:T(8,128)(2,1)S(1)}, u32[]{:S(2)}, u32[]{:S(2)}) %all-to-all-start) | async-done | bytes 1048608 | tf_op jit(solution)/shard_map/all_to_all | solution.py:436
  38.3 0.0 copy-done.4
  38.3 2.8 %shard_map.70 = (bf16[1024,384]{1,0:T(8,128)(2,1)S(1)}, bf16[1024,128]{1,0:T(8,128)(2,1)S(1)}) custom-call(s32[1,8]{1,0:T(1,128)S(1)} %copy-done.4, bf16[8,512,128]{2,1,0:T(8,128)(2,1)S(1)} %all-to-all-done.recv), custom_call_target="tpu_custom_call" | custom-call | tf_op jit(solution)/shard_map/pallas_call | solution.py:309
  41.1 2.4 %collective-permute-start = (bf16[1024,384]{1,0:T(8,128)(2,1)S(1)}, bf16[1024,384]{1,0:T(8,128)(2,1)S(1)}, u32[]{:S(2)}, u32[]{:S(2)}) collective-permute-start(bf16[1024,384]{1,0:T(8,128)(2,1)S(1)} %get-tuple-element.12.packed), channel_id=1, source_target_pairs={{0,64},{64,0},{128,192},{192,128},{256,320},{320,256},{384,448},{4... | collective-permute-start | bytes 2359304 | tf_op jit(solution)/shard_map/ppermute | solution.py:441
  43.5 4.4 %shard_map.71.sent = bf16[64,96,128]{2,1,0:T(8,128)(2,1)S(1)} custom-call(bf16[1024,384]{1,0:T(8,128)(2,1)S(1)} %get-tuple-element.12.packed, bf16[2,1024,1024]{2,1,0:T(8,128)(2,1)} %copy-done.1), custom_call_target="tpu_custom_call" | custom-call | flops 1600000000 | bytes 6000000 | tf_op jit(solution)/shard_map/pallas_call | solution.py:347
  47.9 0.0 collective-permute-done.partner
  47.9 2.0 %shard_map.72 = bf16[64,96,128]{2,1,0:T(8,128)(2,1)S(1)} custom-call(bf16[1024,384]{1,0:T(8,128)(2,1)S(1)} %get-tuple-element.12.packed, bf16[1024,384]{1,0:T(8,128)(2,1)S(1)} %collective-permute-done.partner, bf16[1024,128]{1,0:T(8,128)(2,1)S(1)} %get-tuple-element.13.extras, ...), custom_call_target="tpu_custom_call", output_to_operand_aliasing={{}: (4, {})} | custom-call | tf_op jit(solution)/shard_map/pallas_call | solution.py:389
  49.9 50.1 %all_to_all.10.recv = bf16[64,96,128]{2,1,0:T(8,128)(2,1)S(1)} all-to-all(bf16[64,96,128]{2,1,0:T(8,128)(2,1)S(1)} %shard_map.72), channel_id=1, replica_groups={{56,57,58,59,60,61,62,63,48,49,50,51,52,53,54,55,40,41,42,43,44,45,46,4..., dimensions={0} | all-to-all | bytes 3145728 | tf_op jit(solution)/shard_map/all_to_all | solution.py:444
  100.0 1.5 %shard_map.73 = (bf16[3,64,16,128]{3,2,1,0:T(8,128)(2,1)}, bf16[3,64,16,128]{3,2,1,0:T(8,128)(2,1)}) custom-call(bf16[64,96,128]{2,1,0:T(8,128)(2,1)S(1)} %all_to_all.10.recv), custom_call_target="tpu_custom_call" | custom-call | tf_op jit(solution)/shard_map/pallas_call | solution.py:421
Async XLA Ops:
  3.5 14.0 %copy-start = (f32[4,256,256]{2,1,0:T(8,128)S(1)}, f32[4,256,256]{2,1,0:T(8,128)}, u32[]{:S(2)}) copy-start(f32[4,256,256]{2,1,0:T(8,128)} %inv_x.1) | copy-start | bytes 3145732
  3.5 14.0 %copy-start.2 = (f32[4,256,256]{2,1,0:T(8,128)S(1)}, f32[4,256,256]{2,1,0:T(8,128)}, u32[]{:S(2)}) copy-start(f32[4,256,256]{2,1,0:T(8,128)} %inv_y.1) | copy-start | bytes 3145732
  3.5 14.0 %copy-start.3 = (f32[1024]{0:T(1024)S(1)}, f32[1024]{0:T(1024)}, u32[]{:S(2)}) copy-start(f32[1024]{0:T(1024)} %param.9) | copy-start | bytes 12292
  3.5 34.8 %all-to-all-start = ((bf16[8,512,128]{2,1,0:T(8,128)(2,1)}), bf16[8,512,128]{2,1,0:T(8,128)(2,1)S(1)}, u32[]{:S(2)}, u32[]{:S(2)}) async-start(bf16[8,512,128]{2,1,0:T(8,128)(2,1)} %shard_map.68), calls=%async_computation | async-start | bytes 2097152 | tf_op jit(solution)/shard_map/all_to_all | solution.py:436
  17.4 20.9 %copy-start.4 = (s32[1,8]{1,0:T(1,128)S(1)}, s32[1,8]{1,0:T(1,128)}, u32[]{:S(2)}) copy-start(s32[1,8]{1,0:T(1,128)} %lengths.1) | copy-start | bytes 100
  21.0 1.9 %copy-start.1 = (bf16[2,1024,1024]{2,1,0:T(8,128)(2,1)}, bf16[2,1024,1024]{2,1,0:T(8,128)(2,1)S(1)}, u32[]{:S(2)}) copy-start(bf16[2,1024,1024]{2,1,0:T(8,128)(2,1)S(1)} %get-tuple-element.15.weights_hbm) | copy-start | bytes 12582916
  41.1 6.8 %collective-permute-start = (bf16[1024,384]{1,0:T(8,128)(2,1)S(1)}, bf16[1024,384]{1,0:T(8,128)(2,1)S(1)}, u32[]{:S(2)}, u32[]{:S(2)}) collective-permute-start(bf16[1024,384]{1,0:T(8,128)(2,1)S(1)} %get-tuple-element.12.packed), channel_id=1, source_target_pairs={{0,64},{64,0},{128,192},{192,128},{256,320},{320,256},{384,448},{4... | collective-permute-start | bytes 2359304 | tf_op jit(solution)/shard_map/ppermute | solution.py:441

commit v3 on v2

v3 whole, which is shorter than its diff:
```python
import jax
import jax.numpy as jnp
from jax import lax
from jax.experimental import pallas as pl
from jax.experimental.pallas import tpu as pltpu
from jax.sharding import PartitionSpec as P

A2 = 14.0 / 9.0 / 2.0
B4 = 1.0 / 9.0 / 4.0
ALPHA = 1.0 / 3.0
F32 = jnp.float32
BF16 = jnp.bfloat16
NT = (((1,), (1,)), ((), ()))
MIB = 1 << 20
fixed = pltpu.with_memory_space_constraint
ROW = (5, 4, 1, 0, 7, 6, 3, 2)
COL = (7, 6, 5, 4, 3, 2, 1, 0)
SPANS = ((0, 48), (48, 48), (96, 64))


def lanes(shape):
    return lax.broadcasted_iota(jnp.int32, shape, len(shape) - 1)


def sublanes(shape):
    return lax.broadcasted_iota(jnp.int32, shape, len(shape) - 2)


def split(value):
    high = value.astype(BF16)
    return high, (value - high.astype(F32)).astype(BF16)


def roll(value, shift):
    return pltpu.roll(value, shift % value.shape[-1], value.ndim - 1)


def stencil(rows):
    return A2 * (roll(rows, 1) - roll(rows, -1)) + B4 * (roll(rows, 2) - roll(rows, -2))


def stencil_line(rows):
    width = rows.shape[-1]
    lane = lanes(rows.shape)

    def shifted(by):
        inside = lane >= by if by > 0 else lane < width + by
        return jnp.where(inside, roll(rows, by), 0.0)

    return A2 * (shifted(1) - shifted(-1)) + B4 * (shifted(2) - shifted(-2))


def coupling_rows(first, last, blocks, width):
    total = blocks * width

    def place(row, k):
        parts = []
        if k:
            parts.append(jnp.zeros((1, k * width), F32))
        parts.append(row)
        if k < blocks - 1:
            parts.append(jnp.zeros((1, (blocks - 1 - k) * width), F32))
        return jnp.concatenate(parts, axis=1)

    stacked = jnp.concatenate(
        [place(last[k], k) for k in range(blocks)] + [place(first[k], k) for k in range(blocks)], axis=0
    )
    applied = stencil_line(stacked)
    g_last = []
    for k in range(blocks):
        row = applied[k : k + 1]
        if k:
            row = row - ALPHA * last[k][:, 0:1] * g_last[k - 1]
        g_last.append(row)
    u_first = [None] * blocks
    for k in range(blocks - 1, -1, -1):
        row = applied[blocks + k : blocks + k + 1]
        if k:
            row = row - ALPHA * first[k][:, 0:1] * g_last[k - 1]
        if k < blocks - 1:
            row = row - ALPHA * first[k][:, width - 1 : width] * u_first[k + 1]
        u_first[k] = row
    return g_last, u_first


def functionals(first, last, blocks, width):
    line = blocks * width
    g_last, u_first = coupling_rows(first, last, blocks, width)
    lane = lanes((1, line))
    zero = jnp.zeros((1, line), F32)

    def unit(at):
        return jnp.where(lane == at, 1.0, 0.0)

    rows = []
    for k in range(blocks):
        lo, hi = width * k, width * (k + 1)
        before, after, tip, end = zero, zero, zero, zero
        if k:
            before = -A2 * unit(lo - 1) - B4 * unit(lo - 2) - ALPHA * g_last[k - 1]
            tip = unit(lo - 1)
        if k < blocks - 1:
            after = A2 * unit(hi) + B4 * unit(hi + 1) - ALPHA * u_first[k + 1]
            end = unit(hi)
        rows += [before, before, tip, end, after, after, zero, zero]
    return jnp.concatenate(split(jnp.concatenate(rows, axis=0)), axis=0), g_last, u_first


def coded(value):
    count = value.shape[0] // 2
    value = value[0:count] + value[count : 2 * count]
    top = value.astype(BF16).astype(F32)
    place = sublanes(value.shape) % 8
    return jnp.where((place == 1) | (place == 5), value - top, top)


def edge_columns(tile, lane):
    width = tile.shape[1]
    value = jnp.where((lane == 0) | (lane == 1), tile[:, 0:1], 0.0)
    value = jnp.where(lane == 2, -B4 * tile[:, 1:2], value)
    value = jnp.where(lane == 3, B4 * tile[:, width - 2 : width - 1], value)
    return jnp.where((lane == 4) | (lane == 5), tile[:, width - 1 : width], value)


def pack_kernel(vel_hbm, inv, out, vel, heads, tails, codes, sems, sends):
    blocks, width = inv.shape[0], inv.shape[1]
    line = blocks * width
    copy_heads = pltpu.make_async_copy(inv.at[:, pl.ds(0, 16), :], heads, sems.at[0])
    copy_tails = pltpu.make_async_copy(inv.at[:, pl.ds(width - 16, 16), :], tails, sems.at[1])
    copy_heads.start()
    copy_tails.start()
    comps = vel.shape[0]
    loads, copies = [], []
    for c in range(comps):
        for number, (begin, size) in enumerate(SPANS):
            here = (c, pl.ds(begin, size))
            copy = pltpu.make_async_copy(vel_hbm.at[here], vel.at[here], sems.at[2 + len(SPANS) * c + number])
            copy.start()
            loads.append(copy)
    copy_heads.wait()
    copy_tails.wait()
    first = [heads[k, 0:1, :] for k in range(blocks)]
    last = [tails[k, 15:16, :] for k in range(blocks)]
    both, _, _ = functionals(first, last, blocks, width)
    parts = []
    for c in range(comps):
        for copy in loads[len(SPANS) * c : len(SPANS) * (c + 1)]:
            copy.wait()
        for i in range(out.shape[0]):
            copy = pltpu.make_async_copy(
                vel.at[c, :, pl.ds(128 * ROW[i], 128)], out.at[i, pl.ds(160 * c, 160), :], sends.at[c, i]
            )
            copy.start()
            copies.append(copy)
        parts.append(coded(lax.dot_general(both, vel[c, 0:128, :], NT, preferred_element_type=F32)))
    spare = [vel[c, 128:160, :] for c in range(comps)] + [jnp.zeros((32, line), BF16)]
    spare = jnp.concatenate(spare, axis=0)
    parts.append(coded(lax.dot_general(both, spare, NT, preferred_element_type=F32)))
    for k in range(blocks):
        codes[k] = jnp.concatenate([part[8 * k : 8 * k + 8] for part in parts], axis=0).astype(BF16)
    for i in range(out.shape[0]):
        copy = pltpu.make_async_copy(codes.at[ROW[i] // 2], out.at[i, pl.ds(480, 32), :], sends.at[comps, i])
        copy.start()
        copies.append(copy)
    for copy in copies:
        copy.wait()


def pack(velocity, inverse_x):
    comps, slots, line = velocity.shape
    blocks, width, _ = inverse_x.shape
    return pl.pallas_call(
        pack_kernel,
        out_shape=jax.ShapeDtypeStruct((line // 128, 512, 128), BF16),
        in_specs=[pl.BlockSpec(memory_space=pltpu.HBM), pl.BlockSpec(memory_space=pltpu.HBM)],
        out_specs=pl.BlockSpec(memory_space=pl.ANY),
        scratch_shapes=[
            pltpu.VMEM(velocity.shape, BF16),
            pltpu.VMEM((blocks, 16, width), F32),
            pltpu.VMEM((blocks, 16, width), F32),
            pltpu.VMEM((blocks, 32, 128), BF16),
            pltpu.SemaphoreType.DMA((2 + len(SPANS) * comps,)),
            pltpu.SemaphoreType.DMA((comps + 1, line // 128)),
        ],
        compiler_params=pltpu.CompilerParams(vmem_limit_bytes=24 * MIB),
    )(fixed(velocity, pltpu.HBM), fixed(inverse_x, pltpu.HBM))


def weights_kernel(where, inv_x, inv_y, metric, out_y, out_f, out_x, own, sem):
    blocks, width = inv_y.shape[0], inv_y.shape[1]
    copy = pltpu.make_async_copy(inv_x.at[where[0], pl.ds(where[1] * 128, 128), :], own, sem)
    copy.start()
    first = [inv_y[k, 0:1, :] for k in range(blocks)]
    last = [inv_y[k, width - 1 : width, :] for k in range(blocks)]
    out_f[...], _, _ = functionals(first, last, blocks, width)
    side = jnp.zeros((128, 128), F32)
    lane = lanes((128, 128))
    for k in range(blocks):
        for half in range(width // 128):
            tile = inv_y[k, 128 * half : 128 * half + 128, :]
            inner = stencil(jnp.concatenate([side, tile, side], axis=1))[:, 128 : 128 + width]
            at = k * width + 128 * half
            scale = jnp.broadcast_to(metric[at // 128 : at // 128 + 1, :], (128, 128)).T
            full = jnp.concatenate([inner, edge_columns(tile, lane)], axis=1)
            full = full * jnp.concatenate([scale] * (full.shape[1] // 128), axis=1)
            out_y[0, at : at + 128, :], out_y[1, at : at + 128, :] = split(full)
    copy.wait()
    tile = own[...]
    inner = stencil(jnp.concatenate([side, tile, side], axis=1))
    left, right = inner[:, 128:256], inner[:, 256:384]
    flip = where[1] == 0
    parts = [jnp.where(flip, left, right), jnp.where(flip, right, left)]
    for c in range(3):
        parts.append(edge_columns(tile, lane - 8 * c))
    out_x[0:128, :], out_x[128:256, :] = split(jnp.concatenate(parts, axis=1))


def build_weights(where, inverse_x, inverse_y, metric):
    blocks, width, _ = inverse_y.shape
    size = blocks * width
    vmem = pl.BlockSpec(memory_space=pltpu.VMEM)
    return pl.pallas_call(
        weights_kernel,
        out_shape=(
            jax.ShapeDtypeStruct((2, size, width + 128), BF16),
            jax.ShapeDtypeStruct((16 * blocks, size), BF16),
            jax.ShapeDtypeStruct((256, 640), BF16),
        ),
        in_specs=[pl.BlockSpec(memory_space=pltpu.SMEM), pl.BlockSpec(memory_space=pl.ANY), vmem, vmem],
        out_specs=(vmem, vmem, vmem),
        scratch_shapes=[pltpu.VMEM((128, width), F32), pltpu.SemaphoreType.DMA],
        compiler_params=pltpu.CompilerParams(vmem_limit_bytes=24 * MIB),
        cost_estimate=pl.CostEstimate(flops=20_000_000, bytes_accessed=6_000_000, transcendentals=0),
    )(where, inverse_x, inverse_y, metric)


def target_rows(lengths):
    starts, total = [], jnp.int32(0)
    for s in range(8):
        starts.append(total)
        total = total + lengths[0, s]
    targets = []
    lane = lanes((1, 256))
    for tile in range(5):
        if tile < 4:
            slot, source, names = lane % 128, lane // 128 + 2 * tile, (2 * tile, 2 * tile + 1)
        else:
            slot, source, names = 128 + lane % 32, lane // 32, range(8)
        target = jnp.full((1, 256), -1, jnp.int32)
        for s in names:
            held = (source == s) & (slot < lengths[0, ROW[s]])
            target = jnp.where(held, starts[ROW[s]] + slot, target)
        targets.append(target)
    return jnp.concatenate(targets, axis=1)


def picks(targets, part):
    row = sublanes((256, 1280)) + 256 * part
    return jnp.where(row == targets, 1.0, 0.0).astype(BF16)


def compact_kernel(lengths, recv, weights_hbm, rows_hbm, packed, extras, weights, rows, sems):
    fetches = (
        pltpu.make_async_copy(rows_hbm, rows, sems.at[0]),
        pltpu.make_async_copy(weights_hbm, weights, sems.at[1]),
    )
    for fetch in fetches:
        fetch.start()
    targets = target_rows(lengths)
    small = lanes((8, 128)) // 32
    pad = jnp.zeros((104, 256), F32)
    sent = [recv[s, 480:512, :].astype(F32) for s in range(8)]
    feats = []
    for tile in range(5):
        if tile < 4:
            block = jnp.concatenate([sent[2 * tile][0:24], sent[2 * tile + 1][0:24]], axis=1)
        else:
            halves = []
            for begin in (0, 4):
                lines = []
                for c in range(3):
                    value = jnp.zeros((8, 128), F32)
                    for q in range(4):
                        value = jnp.where(small == q, roll(sent[begin + q][24:32], 32 * (q - c)), value)
                    lines.append(value)
                halves.append(jnp.concatenate(lines, axis=0))
            block = jnp.concatenate(halves, axis=1)
        feats.append(jnp.concatenate([block, pad], axis=0).T.astype(BF16))
    data = []
    for tile in range(5):
        columns = []
        for c in range(3):
            if tile < 4:
                block = recv[2 * tile : 2 * tile + 2, 160 * c : 160 * c + 128, :]
            else:
                block = recv[:, 160 * c + 128 : 160 * c + 160, :]
            columns.append(block.reshape(256, 128))
        data.append(jnp.concatenate(columns + [feats[tile]], axis=1))
    data = jnp.concatenate(data, axis=0)
    for part in range(4):
        here = slice(256 * part, 256 * part + 256)
        value = jnp.dot(picks(targets, part), data, preferred_element_type=F32).astype(BF16)
        packed[here, :] = value[:, 0:384]
        extras[here, :] = value[:, 384:512]
    for fetch in fetches:
        fetch.wait()


def compact(lengths, recv, weights, rows):
    vmem, hbm = pl.BlockSpec(memory_space=pltpu.VMEM), pl.BlockSpec(memory_space=pltpu.HBM)
    return pl.pallas_call(
        compact_kernel,
        out_shape=(
            jax.ShapeDtypeStruct((1024, 384), BF16),
            jax.ShapeDtypeStruct((1024, 128), BF16),
            jax.ShapeDtypeStruct(weights.shape, BF16),
            jax.ShapeDtypeStruct(rows.shape, BF16),
        ),
        in_specs=[pl.BlockSpec(memory_space=pltpu.SMEM), vmem, hbm, hbm],
        out_specs=(vmem, vmem, vmem, vmem),
        scratch_shapes=[pltpu.SemaphoreType.DMA((2,))],
        compiler_params=pltpu.CompilerParams(vmem_limit_bytes=24 * MIB),
    )(lengths, recv, fixed(weights, pltpu.HBM), fixed(rows, pltpu.HBM))


def normal_kernel(packed, weights, rows, out, held, sems):
    field = packed[...]
    edges = coded(jnp.dot(rows[...], field, preferred_element_type=F32))
    spare = jnp.zeros((120, edges.shape[1]), F32)
    copies = []
    for part in range(4):
        here = slice(256 * part, 256 * part + 256)
        edge = jnp.concatenate([edges[8 * part : 8 * part + 8], spare], axis=0).astype(BF16)
        block = jnp.concatenate([field[here], edge], axis=0)
        value = jnp.dot(weights[0, here, :], block, preferred_element_type=F32)
        value = value + jnp.dot(weights[1, here, :], block, preferred_element_type=F32)
        for c in range(3):
            block = value[:, 128 * c : 128 * c + 128].astype(BF16).reshape(16, 16, 128)
            for half in range(2):
                at = 8 * COL.index(2 * part + half)
                held[at : at + 8, 16 * c : 16 * c + 16, :] = block[8 * half : 8 * half + 8]
        for half in range(2):
            runs = pl.ds(8 * COL.index(2 * part + half), 8)
            copy = pltpu.make_async_copy(
                held.at[runs], out.at[runs, pl.ds(48, 48), :], sems.at[2 * part + half]
            )
            copy.start()
            copies.append(copy)
    for copy in copies:
        copy.wait()


def normal(packed, weights, rows):
    vmem = pl.BlockSpec(memory_space=pltpu.VMEM)
    return pl.pallas_call(
        normal_kernel,
        out_shape=jax.ShapeDtypeStruct((64, 96, 128), BF16),
        in_specs=[vmem, vmem, vmem],
        out_specs=pl.BlockSpec(memory_space=pl.ANY),
        scratch_shapes=[pltpu.VMEM((64, 48, 128), BF16), pltpu.SemaphoreType.DMA((8,))],
        compiler_params=pltpu.CompilerParams(vmem_limit_bytes=24 * MIB),
        cost_estimate=pl.CostEstimate(flops=1_600_000_000, bytes_accessed=6_000_000, transcendentals=0),
    )(packed, weights, rows)


def stream_kernel(packed, partner, extras, weights, sent, out, held, sems):
    del sent
    copies = []
    for c in range(3):
        columns = slice(128 * c, 128 * c + 128)
        field = jnp.concatenate([packed[:, columns], partner[:, columns], extras[...]], axis=1)
        matrix = jnp.concatenate(
            [weights[:, 0:256], weights[:, 256 + 128 * c : 384 + 128 * c]], axis=1
        )
        value = lax.dot_general(field, matrix, NT, preferred_element_type=F32)
        value = value[:, 0:128] + value[:, 128:256]
        rows = pl.ds(16 * c, 16)
        block = value.astype(BF16).reshape(64, 16, 128)
        for run in range(8):
            at = 8 * COL.index(run)
            held[at : at + 8, 16 * c : 16 * c + 16, :] = block[8 * run : 8 * run + 8]
        copy = pltpu.make_async_copy(held.at[:, rows, :], out.at[:, rows, :], sems.at[c])
        copy.start()
        copies.append(copy)
    for copy in copies:
        copy.wait()


def stream(packed, partner, extras, weights, sent):
    vmem = pl.BlockSpec(memory_space=pltpu.VMEM)
    return pl.pallas_call(
        stream_kernel,
        out_shape=jax.ShapeDtypeStruct((64, 96, 128), BF16),
        in_specs=[vmem, vmem, vmem, vmem, pl.BlockSpec(memory_space=pl.ANY)],
        out_specs=pl.BlockSpec(memory_space=pl.ANY),
        scratch_shapes=[pltpu.VMEM((64, 48, 128), BF16), pltpu.SemaphoreType.DMA((4,))],
        input_output_aliases={4: 0},
        compiler_params=pltpu.CompilerParams(vmem_limit_bytes=24 * MIB),
    )(packed, partner, extras, weights, sent)


def unpack_kernel(recv, out_x, out_y, sems):
    copies = []
    for which, out in enumerate((out_x, out_y)):
        for c in range(3):
            for run in range(8):
                copies.append(
                    pltpu.make_async_copy(
                        recv.at[pl.ds(8 * COL.index(run), 8), pl.ds(48 * which + 16 * c, 16), :],
                        out.at[c, pl.ds(8 * run, 8)],
                        sems.at[3 * which + c, run],
                    )
                )
    for copy in copies:
        copy.start()
    for copy in copies:
        copy.wait()


def unpack(recv):
    shape = jax.ShapeDtypeStruct((3, 64, 16, 128), BF16)
    anywhere = pl.BlockSpec(memory_space=pl.ANY)
    return pl.pallas_call(
        unpack_kernel,
        out_shape=(shape, shape),
        in_specs=[anywhere],
        out_specs=(anywhere, anywhere),
        scratch_shapes=[pltpu.SemaphoreType.DMA((6, 8))],
        compiler_params=pltpu.CompilerParams(vmem_limit_bytes=16 * MIB),
    )(recv)


def local(velocity, lengths, inverse_x, inverse_y, metric):
    rank = lax.axis_index("row")
    where = jnp.stack([lax.shift_right_logical(rank, 1), rank & 1]).astype(jnp.int32)
    sent = pack(velocity[:, 0], inverse_x)
    weights = build_weights(where, inverse_x, inverse_y, metric.reshape(8, 128))
    received = lax.all_to_all(
        sent, "row", split_axis=0, concat_axis=0, tiled=True, axis_index_groups=[list(ROW)]
    )
    received, (weights_y, rows, weights_x) = lax.optimization_barrier((received, weights))
    packed, extras, weights_y, rows = compact(lengths, received, weights_y, rows)
    partner = lax.ppermute(packed, "row", [(i, i ^ 1) for i in range(8)])
    result = normal(packed, weights_y, rows)
    result = stream(packed, partner, extras, weights_x, result)
    moved = lax.all_to_all(
        result,
        "col",
        split_axis=0,
        concat_axis=0,
        tiled=True,
        axis_index_groups=[[8 * run + i for run in COL for i in range(8)]],
    )
    return unpack(moved)


def solution(mesh):
    return jax.shard_map(
        local,
        mesh=mesh,
        in_specs=(P(None, "col", "row", None), P("col", None), P(), P(), P()),
        out_specs=(P(None, None, "col", "row"), P(None, None, "col", "row")),
        check_vma=False,
    )
```

time: 102 us -> 98.5 us (0.966)
  Pallas kernels: 17 us -> 13.9 us
    pallas_call x1, Pallas kernels: 4.38 us -> 2.15 us  [normal(): pl.pallas_call(normal_kernel, out_shape=jax.ShapeDtypeStruct((64, 96, 128...]
  transfers between devices with their start and end apart: 2 -> 2, of which waited for: 1 -> 1; matrix products, arithmetic and copies ran while one was open for 0% -> 0% of each run, Pallas kernels for 8% -> 5%
where the time goes in v3:
time: 98.5 us; the launch traced here: 98.2 us
  blocking collectives  50.1 us (51%)
  starting transfers between devices  16 us (16%)
  waiting for transfers between devices  15.5 us (16%)
  Pallas kernels  13.9 us (14%)
  local copies, waits for them, and re-layouts  1.82 us (2%)
    all_to_all x1, blocking collectives, local(): lax.all_to_all(result, 'col', split_axis=0, concat_axis=0, tiled=True, ax...  50.1 us
    all_to_all x1, waiting for transfers between devices, local(): lax.all_to_all(sent, 'row', split_axis=0, concat_axis=0, tiled=True, axis...  15.5 us
    all_to_all x1, starting transfers between devices, local(): lax.all_to_all(sent, 'row', split_axis=0, concat_axis=0, tiled=True, axis...  13.6 us
    pallas_call x1, Pallas kernels, build_weights(): pl.pallas_call(weights_kernel, out_shape=(jax.ShapeDtypeStruct((2, size,...  3.04 us
    pallas_call x1, Pallas kernels, pack(): pl.pallas_call(pack_kernel, out_shape=jax.ShapeDtypeStruct((line // 128,...  2.95 us
    ppermute x1, starting transfers between devices, local(): partner = lax.ppermute(packed, 'row', [(i, i ^ 1) for i in range(8)])  2.46 us
    pallas_call x1, Pallas kernels, compact(): pl.pallas_call(compact_kernel, out_shape=(jax.ShapeDtypeStruct((1024, 384...  2.2 us
    pallas_call x1, Pallas kernels, normal(): pl.pallas_call(normal_kernel, out_shape=jax.ShapeDtypeStruct((64, 96, 128...  2.15 us
  transfers between devices with their start and end apart: 2, of which 1 were waited for; matrix products, arithmetic and copies ran while one was open for 0% of the time, Pallas kernels for 5%

profile of v3, /device:TPU:1, one launch (start us, length us, event | category | flops | bytes accessed | tf_op | source)
XLA Modules:
  0.0 98.2 jit_solution(2074013393794203752)
XLA Ops:
  0.6 2.9 %shard_map.68 = bf16[8,512,128]{2,1,0:T(8,128)(2,1)} custom-call(bf16[3,160,1024]{2,1,0:T(8,128)(2,1)} %bitcast.5, f32[4,256,256]{2,1,0:T(8,128)} %inv_x.1), custom_call_target="tpu_custom_call" | custom-call | tf_op jit(solution)/shard_map/pallas_call | solution.py:172
  3.6 0.0 copy-start
  3.6 0.0 copy-start.2
  3.6 0.0 copy-start.4
  3.6 13.6 %all-to-all-start = ((bf16[8,512,128]{2,1,0:T(8,128)(2,1)}), bf16[8,512,128]{2,1,0:T(8,128)(2,1)S(1)}, u32[]{:S(2)}, u32[]{:S(2)}) async-start(bf16[8,512,128]{2,1,0:T(8,128)(2,1)} %shard_map.68), calls=%async_computation | async-start | bytes 2097152 | tf_op jit(solution)/shard_map/all_to_all | solution.py:438
  17.2 0.0 copy-start.5
  17.2 0.1 pad_add_fusion.where
  17.2 0.0 copy-done
  17.3 0.0 copy-done.2
  17.3 0.0 copy-done.4
  17.3 3.0 %shard_map.69 = (bf16[2,1024,384]{2,1,0:T(8,128)(2,1)S(1)}, bf16[64,1024]{1,0:T(8,128)(2,1)S(1)}, bf16[256,640]{1,0:T(8,128)(2,1)S(1)}) custom-call(s32[2]{0:T(128)S(1)} %pad_add_fusion.where, f32[4,256,256]{2,1,0:T(8,128)S(1)} %copy-done, f32[4,256,256]{2,1,0:T(8,128)S(1)} %copy-done.2, f32[8,128]{1,0:T(8,128)S(1)} %bitcast.4), custom_call_target="tpu_custom_call" | custom-call | flops 20000000 | bytes 6000000 | tf_op jit(solution)/shard_map/pallas_call | solution.py:222
  20.3 0.0 copy-start.1
  20.3 1.1 %copy-done.1 = bf16[2,1024,384]{2,1,0:T(8,128)(2,1)} copy-done((bf16[2,1024,384]{2,1,0:T(8,128)(2,1)}, bf16[2,1024,384]{2,1,0:T(8,128)(2,1)S(1)}, u32[]{:S(2)}) %copy-start.1) | copy-done | bytes 1572888
  21.5 0.0 copy-start.3
  21.5 0.7 copy-done.3
  22.1 15.5 %all-to-all-done.recv = bf16[8,512,128]{2,1,0:T(8,128)(2,1)S(1)} async-done(((bf16[8,512,128]{2,1,0:T(8,128)(2,1)}), bf16[8,512,128]{2,1,0:T(8,128)(2,1)S(1)}, u32[]{:S(2)}, u32[]{:S(2)}) %all-to-all-start) | async-done | bytes 1048608 | tf_op jit(solution)/shard_map/all_to_all | solution.py:438
  37.6 0.0 copy-done.5
  37.6 2.2 %shard_map.70 = (bf16[1024,384]{1,0:T(8,128)(2,1)S(1)}, bf16[1024,128]{1,0:T(8,128)(2,1)S(1)}, bf16[2,1024,384]{2,1,0:T(8,128)(2,1)S(1)}, bf16[64,1024]{1,0:T(8,128)(2,1)S(1)}) custom-call(s32[1,8]{1,0:T(1,128)S(1)} %copy-done.5, bf16[8,512,128]{2,1,0:T(8,128)(2,1)S(1)} %all-to-all-done.recv, bf16[2,1024,384]{2,1,0:T(8,128)(2,1)} %copy-done.1, ...), custom_call_target="tpu_custom_call" | custom-call | tf_op jit(solution)/shard_map/pallas_call | solution.py:311
  39.9 2.5 %collective-permute-start = (bf16[1024,384]{1,0:T(8,128)(2,1)S(1)}, bf16[1024,384]{1,0:T(8,128)(2,1)S(1)}, u32[]{:S(2)}, u32[]{:S(2)}) collective-permute-start(bf16[1024,384]{1,0:T(8,128)(2,1)S(1)} %get-tuple-element.19.packed), channel_id=1, source_target_pairs={{0,64},{64,0},{128,192},{192,128},{256,320},{320,256},{384,448},{4... | collective-permute-start | bytes 2359304 | tf_op jit(solution)/shard_map/ppermute | solution.py:443
  42.3 2.1 %shard_map.71.sent = bf16[64,96,128]{2,1,0:T(8,128)(2,1)S(1)} custom-call(bf16[1024,384]{1,0:T(8,128)(2,1)S(1)} %get-tuple-element.19.packed, bf16[2,1024,384]{2,1,0:T(8,128)(2,1)S(1)} %get-tuple-element.22.weights, bf16[64,1024]{1,0:T(8,128)(2,1)S(1)} %get-tuple-element.23.rows), custom_call_target="tpu_custom_call" | custom-call | flops 1600000000 | bytes 6000000 | tf_op jit(solution)/shard_map/pallas_call | solution.py:355
  44.5 0.0 collective-permute-done.partner
  44.5 2.0 %shard_map.72 = bf16[64,96,128]{2,1,0:T(8,128)(2,1)S(1)} custom-call(bf16[1024,384]{1,0:T(8,128)(2,1)S(1)} %get-tuple-element.19.packed, bf16[1024,384]{1,0:T(8,128)(2,1)S(1)} %collective-permute-done.partner, bf16[1024,128]{1,0:T(8,128)(2,1)S(1)} %get-tuple-element.20.extras, ...), custom_call_target="tpu_custom_call", output_to_operand_aliasing={{}: (4, {})} | custom-call | tf_op jit(solution)/shard_map/pallas_call | solution.py:391
  46.5 50.1 %all_to_all.10.recv = bf16[64,96,128]{2,1,0:T(8,128)(2,1)S(1)} all-to-all(bf16[64,96,128]{2,1,0:T(8,128)(2,1)S(1)} %shard_map.72), channel_id=1, replica_groups={{56,57,58,59,60,61,62,63,48,49,50,51,52,53,54,55,40,41,42,43,44,45,46,4..., dimensions={0} | all-to-all | bytes 3145728 | tf_op jit(solution)/shard_map/all_to_all | solution.py:446
  96.7 1.5 %shard_map.73 = (bf16[3,64,16,128]{3,2,1,0:T(8,128)(2,1)}, bf16[3,64,16,128]{3,2,1,0:T(8,128)(2,1)}) custom-call(bf16[64,96,128]{2,1,0:T(8,128)(2,1)S(1)} %all_to_all.10.recv), custom_call_target="tpu_custom_call" | custom-call | tf_op jit(solution)/shard_map/pallas_call | solution.py:423
Async XLA Ops:
  3.6 13.7 %copy-start = (f32[4,256,256]{2,1,0:T(8,128)S(1)}, f32[4,256,256]{2,1,0:T(8,128)}, u32[]{:S(2)}) copy-start(f32[4,256,256]{2,1,0:T(8,128)} %inv_x.1) | copy-start | bytes 3145732
  3.6 13.7 %copy-start.2 = (f32[4,256,256]{2,1,0:T(8,128)S(1)}, f32[4,256,256]{2,1,0:T(8,128)}, u32[]{:S(2)}) copy-start(f32[4,256,256]{2,1,0:T(8,128)} %inv_y.1) | copy-start | bytes 3145732
  3.6 13.6 %copy-start.4 = (f32[1024]{0:T(1024)S(1)}, f32[1024]{0:T(1024)}, u32[]{:S(2)}) copy-start(f32[1024]{0:T(1024)} %param.9) | copy-start | bytes 12292
  3.6 34.0 %all-to-all-start = ((bf16[8,512,128]{2,1,0:T(8,128)(2,1)}), bf16[8,512,128]{2,1,0:T(8,128)(2,1)S(1)}, u32[]{:S(2)}, u32[]{:S(2)}) async-start(bf16[8,512,128]{2,1,0:T(8,128)(2,1)} %shard_map.68), calls=%async_computation | async-start | bytes 2097152 | tf_op jit(solution)/shard_map/all_to_all | solution.py:438
  17.2 20.5 %copy-start.5 = (s32[1,8]{1,0:T(1,128)S(1)}, s32[1,8]{1,0:T(1,128)}, u32[]{:S(2)}) copy-start(s32[1,8]{1,0:T(1,128)} %lengths.1) | copy-start | bytes 100
  20.3 1.2 %copy-start.1 = (bf16[2,1024,384]{2,1,0:T(8,128)(2,1)}, bf16[2,1024,384]{2,1,0:T(8,128)(2,1)S(1)}, u32[]{:S(2)}) copy-start(bf16[2,1024,384]{2,1,0:T(8,128)(2,1)S(1)} %get-tuple-element.17.weights_hbm) | copy-start | bytes 4718596
  21.5 0.7 copy-start.3
  39.9 4.6 %collective-permute-start = (bf16[1024,384]{1,0:T(8,128)(2,1)S(1)}, bf16[1024,384]{1,0:T(8,128)(2,1)S(1)}, u32[]{:S(2)}, u32[]{:S(2)}) collective-permute-start(bf16[1024,384]{1,0:T(8,128)(2,1)S(1)} %get-tuple-element.19.packed), channel_id=1, source_target_pairs={{0,64},{64,0},{128,192},{192,128},{256,320},{320,256},{384,448},{4... | collective-permute-start | bytes 2359304 | tf_op jit(solution)/shard_map/ppermute | solution.py:443

commit v4 on v3

--- a/solution.py
+++ b/solution.py
@@ -15,7 +15,7 @@
 fixed = pltpu.with_memory_space_constraint
 ROW = (5, 4, 1, 0, 7, 6, 3, 2)
 COL = (7, 6, 5, 4, 3, 2, 1, 0)
-SPANS = ((0, 48), (48, 48), (96, 64))
+SPANS = ((0, 160),)
 
 
 def lanes(shape):
@@ -323,11 +323,10 @@
     )(lengths, recv, fixed(weights, pltpu.HBM), fixed(rows, pltpu.HBM))
 
 
-def normal_kernel(packed, weights, rows, out, held, sems):
+def normal_kernel(packed, weights, rows, out):
     field = packed[...]
     edges = coded(jnp.dot(rows[...], field, preferred_element_type=F32))
     spare = jnp.zeros((120, edges.shape[1]), F32)
-    copies = []
     for part in range(4):
         here = slice(256 * part, 256 * part + 256)
         edge = jnp.concatenate([edges[8 * part : 8 * part + 8], spare], axis=0).astype(BF16)
@@ -338,34 +337,22 @@
             block = value[:, 128 * c : 128 * c + 128].astype(BF16).reshape(16, 16, 128)
             for half in range(2):
                 at = 8 * COL.index(2 * part + half)
-                held[at : at + 8, 16 * c : 16 * c + 16, :] = block[8 * half : 8 * half + 8]
-        for half in range(2):
-            runs = pl.ds(8 * COL.index(2 * part + half), 8)
-            copy = pltpu.make_async_copy(
-                held.at[runs], out.at[runs, pl.ds(48, 48), :], sems.at[2 * part + half]
-            )
-            copy.start()
-            copies.append(copy)
-    for copy in copies:
-        copy.wait()
+                out[at : at + 8, 16 * c : 16 * c + 16, :] = block[8 * half : 8 * half + 8]
 
 
 def normal(packed, weights, rows):
     vmem = pl.BlockSpec(memory_space=pltpu.VMEM)
     return pl.pallas_call(
         normal_kernel,
-        out_shape=jax.ShapeDtypeStruct((64, 96, 128), BF16),
+        out_shape=jax.ShapeDtypeStruct((64, 48, 128), BF16),
         in_specs=[vmem, vmem, vmem],
-        out_specs=pl.BlockSpec(memory_space=pl.ANY),
-        scratch_shapes=[pltpu.VMEM((64, 48, 128), BF16), pltpu.SemaphoreType.DMA((8,))],
+        out_specs=vmem,
         compiler_params=pltpu.CompilerParams(vmem_limit_bytes=24 * MIB),
         cost_estimate=pl.CostEstimate(flops=1_600_000_000, bytes_accessed=6_000_000, transcendentals=0),
     )(packed, weights, rows)
 
 
-def stream_kernel(packed, partner, extras, weights, sent, out, held, sems):
-    del sent
-    copies = []
+def stream_kernel(packed, partner, extras, weights, sent, out):
     for c in range(3):
         columns = slice(128 * c, 128 * c + 128)
         field = jnp.concatenate([packed[:, columns], partner[:, columns], extras[...]], axis=1)
@@ -374,16 +361,11 @@
         )
         value = lax.dot_general(field, matrix, NT, preferred_element_type=F32)
         value = value[:, 0:128] + value[:, 128:256]
-        rows = pl.ds(16 * c, 16)
         block = value.astype(BF16).reshape(64, 16, 128)
         for run in range(8):
             at = 8 * COL.index(run)
-            held[at : at + 8, 16 * c : 16 * c + 16, :] = block[8 * run : 8 * run + 8]
-        copy = pltpu.make_async_copy(held.at[:, rows, :], out.at[:, rows, :], sems.at[c])
-        copy.start()
-        copies.append(copy)
-    for copy in copies:
-        copy.wait()
+            out[at : at + 8, 16 * c : 16 * c + 16, :] = block[8 * run : 8 * run + 8]
+        out[:, 48 + 16 * c : 64 + 16 * c, :] = sent[:, 16 * c : 16 * c + 16, :]
 
 
 def stream(packed, partner, extras, weights, sent):
@@ -391,28 +373,23 @@
     return pl.pallas_call(
         stream_kernel,
         out_shape=jax.ShapeDtypeStruct((64, 96, 128), BF16),
-        in_specs=[vmem, vmem, vmem, vmem, pl.BlockSpec(memory_space=pl.ANY)],
-        out_specs=pl.BlockSpec(memory_space=pl.ANY),
-        scratch_shapes=[pltpu.VMEM((64, 48, 128), BF16), pltpu.SemaphoreType.DMA((4,))],
-        input_output_aliases={4: 0},
+        in_specs=[vmem] * 5,
+        out_specs=vmem,
         compiler_params=pltpu.CompilerParams(vmem_limit_bytes=24 * MIB),
     )(packed, partner, extras, weights, sent)
 
 
-def unpack_kernel(recv, out_x, out_y, sems):
+def unpack_kernel(recv, out_x, out_y, held, sems):
     copies = []
     for which, out in enumerate((out_x, out_y)):
         for c in range(3):
+            at = 48 * which + 16 * c
             for run in range(8):
-                copies.append(
-                    pltpu.make_async_copy(
-                        recv.at[pl.ds(8 * COL.index(run), 8), pl.ds(48 * which + 16 * c, 16), :],
-                        out.at[c, pl.ds(8 * run, 8)],
-                        sems.at[3 * which + c, run],
-                    )
-                )
-    for copy in copies:
-        copy.start()
+                begin = 8 * COL.index(run)
+                held[which, c, 8 * run : 8 * run + 8] = recv[begin : begin + 8, at : at + 16, :]
+            copy = pltpu.make_async_copy(held.at[which, c], out.at[c], sems.at[3 * which + c])
+            copy.start()
+            copies.append(copy)
     for copy in copies:
         copy.wait()
 
@@ -423,10 +400,10 @@
     return pl.pallas_call(
         unpack_kernel,
         out_shape=(shape, shape),
-        in_specs=[anywhere],
+        in_specs=[pl.BlockSpec(memory_space=pltpu.VMEM)],
         out_specs=(anywhere, anywhere),
-        scratch_shapes=[pltpu.SemaphoreType.DMA((6, 8))],
-        compiler_params=pltpu.CompilerParams(vmem_limit_bytes=16 * MIB),
+        scratch_shapes=[pltpu.VMEM((2, 3, 64, 16, 128), BF16), pltpu.SemaphoreType.DMA((6,))],
+        compiler_params=pltpu.CompilerParams(vmem_limit_bytes=24 * MIB),
     )(recv)
 
 

time: 98.5 us -> 96.8 us (0.983)
  Pallas kernels: 13.9 us -> 11.7 us
    pallas_call x2, Pallas kernels: 3.68 us -> 2.54 us  [the longest x1 1.34 us: normal(): pl.pallas_call(normal_kernel, out_shape=jax.ShapeDtypeStruct((64, 48, 128...]
  transfers between devices with their start and end apart: 2 -> 2, of which waited for: 1 -> 2; matrix products, arithmetic and copies ran while one was open for 0% -> 0% of each run, Pallas kernels for 5% -> 5%
where the time goes in v4:
time: 96.8 us; the launch traced here: 95.8 us
  blocking collectives  49.4 us (51%)
  waiting for transfers between devices  16.1 us (17%)
  starting transfers between devices  16 us (17%)
  Pallas kernels  11.7 us (12%)
  local copies, waits for them, and re-layouts  1.82 us (2%)
    all_to_all x1, blocking collectives, local(): lax.all_to_all(result, 'col', split_axis=0, concat_axis=0, tiled=True, ax...  49.4 us
    all_to_all x1, waiting for transfers between devices, local(): lax.all_to_all(sent, 'row', split_axis=0, concat_axis=0, tiled=True, axis...  15.6 us
    all_to_all x1, starting transfers between devices, local(): lax.all_to_all(sent, 'row', split_axis=0, concat_axis=0, tiled=True, axis...  13.6 us
    pallas_call x1, Pallas kernels, build_weights(): pl.pallas_call(weights_kernel, out_shape=(jax.ShapeDtypeStruct((2, size,...  3.04 us
    pallas_call x1, Pallas kernels, pack(): pl.pallas_call(pack_kernel, out_shape=jax.ShapeDtypeStruct((line // 128,...  2.88 us
    ppermute x1, starting transfers between devices, local(): partner = lax.ppermute(packed, 'row', [(i, i ^ 1) for i in range(8)])  2.41 us
    pallas_call x1, Pallas kernels, compact(): pl.pallas_call(compact_kernel, out_shape=(jax.ShapeDtypeStruct((1024, 384...  2.2 us
  transfers between devices with their start and end apart: 2, of which 2 were waited for; matrix products, arithmetic and copies ran while one was open for 0% of the time, Pallas kernels for 5%

profile of v4, /device:TPU:1, one launch (start us, length us, event | category | flops | bytes accessed | tf_op | source)
XLA Modules:
  0.0 95.8 jit_solution(17962717197750322471)
XLA Ops:
  0.6 2.9 %shard_map.68 = bf16[8,512,128]{2,1,0:T(8,128)(2,1)} custom-call(bf16[3,160,1024]{2,1,0:T(8,128)(2,1)} %bitcast.5, f32[4,256,256]{2,1,0:T(8,128)} %inv_x.1), custom_call_target="tpu_custom_call" | custom-call | tf_op jit(solution)/shard_map/pallas_call | solution.py:172
  3.5 0.0 copy-start
  3.5 0.0 copy-start.2
  3.5 0.0 copy-start.4
  3.6 13.6 %all-to-all-start = ((bf16[8,512,128]{2,1,0:T(8,128)(2,1)}), bf16[8,512,128]{2,1,0:T(8,128)(2,1)S(1)}, u32[]{:S(2)}, u32[]{:S(2)}) async-start(bf16[8,512,128]{2,1,0:T(8,128)(2,1)} %shard_map.68), calls=%async_computation | async-start | bytes 2097152 | tf_op jit(solution)/shard_map/all_to_all | solution.py:415
  17.1 0.0 copy-start.5
  17.1 0.1 pad_add_fusion.where
  17.2 0.0 copy-done
  17.2 0.0 copy-done.2
  17.2 0.0 copy-done.4
  17.2 3.0 %shard_map.69 = (bf16[2,1024,384]{2,1,0:T(8,128)(2,1)S(1)}, bf16[64,1024]{1,0:T(8,128)(2,1)S(1)}, bf16[256,640]{1,0:T(8,128)(2,1)S(1)}) custom-call(s32[2]{0:T(128)S(1)} %pad_add_fusion.where, f32[4,256,256]{2,1,0:T(8,128)S(1)} %copy-done, f32[4,256,256]{2,1,0:T(8,128)S(1)} %copy-done.2, f32[8,128]{1,0:T(8,128)S(1)} %bitcast.4), custom_call_target="tpu_custom_call" | custom-call | flops 20000000 | bytes 6000000 | tf_op jit(solution)/shard_map/pallas_call | solution.py:222
  20.2 0.0 copy-start.1
  20.2 1.1 %copy-done.1 = bf16[2,1024,384]{2,1,0:T(8,128)(2,1)} copy-done((bf16[2,1024,384]{2,1,0:T(8,128)(2,1)}, bf16[2,1024,384]{2,1,0:T(8,128)(2,1)S(1)}, u32[]{:S(2)}) %copy-start.1) | copy-done | bytes 1572888
  21.4 0.0 copy-start.3
  21.4 0.7 copy-done.3
  22.0 15.6 %all-to-all-done.recv = bf16[8,512,128]{2,1,0:T(8,128)(2,1)S(1)} async-done(((bf16[8,512,128]{2,1,0:T(8,128)(2,1)}), bf16[8,512,128]{2,1,0:T(8,128)(2,1)S(1)}, u32[]{:S(2)}, u32[]{:S(2)}) %all-to-all-start) | async-done | bytes 1048608 | tf_op jit(solution)/shard_map/all_to_all | solution.py:415
  37.6 0.0 copy-done.5
  37.6 2.2 %shard_map.70 = (bf16[1024,384]{1,0:T(8,128)(2,1)S(1)}, bf16[1024,128]{1,0:T(8,128)(2,1)S(1)}, bf16[2,1024,384]{2,1,0:T(8,128)(2,1)S(1)}, bf16[64,1024]{1,0:T(8,128)(2,1)S(1)}) custom-call(s32[1,8]{1,0:T(1,128)S(1)} %copy-done.5, bf16[8,512,128]{2,1,0:T(8,128)(2,1)S(1)} %all-to-all-done.recv, bf16[2,1024,384]{2,1,0:T(8,128)(2,1)} %copy-done.1, ...), custom_call_target="tpu_custom_call" | custom-call | tf_op jit(solution)/shard_map/pallas_call | solution.py:311
  39.9 2.4 %collective-permute-start = (bf16[1024,384]{1,0:T(8,128)(2,1)S(1)}, bf16[1024,384]{1,0:T(8,128)(2,1)S(1)}, u32[]{:S(2)}, u32[]{:S(2)}) collective-permute-start(bf16[1024,384]{1,0:T(8,128)(2,1)S(1)} %get-tuple-element.19.packed), channel_id=1, source_target_pairs={{0,64},{64,0},{128,192},{192,128},{256,320},{320,256},{384,448},{4... | collective-permute-start | bytes 2359304 | tf_op jit(solution)/shard_map/ppermute | solution.py:420
  42.3 1.3 %shard_map.71.sent = bf16[64,48,128]{2,1,0:T(8,128)(2,1)S(1)} custom-call(bf16[1024,384]{1,0:T(8,128)(2,1)S(1)} %get-tuple-element.19.packed, bf16[2,1024,384]{2,1,0:T(8,128)(2,1)S(1)} %get-tuple-element.22.weights, bf16[64,1024]{1,0:T(8,128)(2,1)S(1)} %get-tuple-element.23.rows), custom_call_target="tpu_custom_call" | custom-call | flops 1600000000 | bytes 6000000 | tf_op jit(solution)/shard_map/pallas_call | solution.py:345
  43.6 0.5 collective-permute-done.partner
  44.2 1.1 %shard_map.72 = bf16[64,96,128]{2,1,0:T(8,128)(2,1)S(1)} custom-call(bf16[1024,384]{1,0:T(8,128)(2,1)S(1)} %get-tuple-element.19.packed, bf16[1024,384]{1,0:T(8,128)(2,1)S(1)} %collective-permute-done.partner, bf16[1024,128]{1,0:T(8,128)(2,1)S(1)} %get-tuple-element.20.extras, bf16[256,640]{1,0:T(8,128)(2,1)S(1)} %get-tuple-element.21.weights, ...), custom_call_target="tpu_custom_call" | custom-call | tf_op jit(solution)/shard_map/pallas_call | solution.py:373
  45.2 49.4 %all_to_all.10.recv = bf16[64,96,128]{2,1,0:T(8,128)(2,1)S(1)} all-to-all(bf16[64,96,128]{2,1,0:T(8,128)(2,1)S(1)} %shard_map.72), channel_id=1, replica_groups={{56,57,58,59,60,61,62,63,48,49,50,51,52,53,54,55,40,41,42,43,44,45,46,4..., dimensions={0} | all-to-all | bytes 3145728 | tf_op jit(solution)/shard_map/all_to_all | solution.py:423
  94.6 1.2 %shard_map.73 = (bf16[3,64,16,128]{3,2,1,0:T(8,128)(2,1)}, bf16[3,64,16,128]{3,2,1,0:T(8,128)(2,1)}) custom-call(bf16[64,96,128]{2,1,0:T(8,128)(2,1)S(1)} %all_to_all.10.recv), custom_call_target="tpu_custom_call" | custom-call | tf_op jit(solution)/shard_map/pallas_call | solution.py:400
Async XLA Ops:
  3.5 13.7 %copy-start = (f32[4,256,256]{2,1,0:T(8,128)S(1)}, f32[4,256,256]{2,1,0:T(8,128)}, u32[]{:S(2)}) copy-start(f32[4,256,256]{2,1,0:T(8,128)} %inv_x.1) | copy-start | bytes 3145732
  3.5 13.7 %copy-start.2 = (f32[4,256,256]{2,1,0:T(8,128)S(1)}, f32[4,256,256]{2,1,0:T(8,128)}, u32[]{:S(2)}) copy-start(f32[4,256,256]{2,1,0:T(8,128)} %inv_y.1) | copy-start | bytes 3145732
  3.5 13.6 %copy-start.4 = (f32[1024]{0:T(1024)S(1)}, f32[1024]{0:T(1024)}, u32[]{:S(2)}) copy-start(f32[1024]{0:T(1024)} %param.9) | copy-start | bytes 12292
  3.6 34.1 %all-to-all-start = ((bf16[8,512,128]{2,1,0:T(8,128)(2,1)}), bf16[8,512,128]{2,1,0:T(8,128)(2,1)S(1)}, u32[]{:S(2)}, u32[]{:S(2)}) async-start(bf16[8,512,128]{2,1,0:T(8,128)(2,1)} %shard_map.68), calls=%async_computation | async-start | bytes 2097152 | tf_op jit(solution)/shard_map/all_to_all | solution.py:415
  17.1 20.5 %copy-start.5 = (s32[1,8]{1,0:T(1,128)S(1)}, s32[1,8]{1,0:T(1,128)}, u32[]{:S(2)}) copy-start(s32[1,8]{1,0:T(1,128)} %lengths.1) | copy-start | bytes 100
  20.2 1.2 %copy-start.1 = (bf16[2,1024,384]{2,1,0:T(8,128)(2,1)}, bf16[2,1024,384]{2,1,0:T(8,128)(2,1)S(1)}, u32[]{:S(2)}) copy-start(bf16[2,1024,384]{2,1,0:T(8,128)(2,1)S(1)} %get-tuple-element.17.weights_hbm) | copy-start | bytes 4718596
  21.4 0.7 copy-start.3
  39.9 4.3 %collective-permute-start = (bf16[1024,384]{1,0:T(8,128)(2,1)S(1)}, bf16[1024,384]{1,0:T(8,128)(2,1)S(1)}, u32[]{:S(2)}, u32[]{:S(2)}) collective-permute-start(bf16[1024,384]{1,0:T(8,128)(2,1)S(1)} %get-tuple-element.19.packed), channel_id=1, source_target_pairs={{0,64},{64,0},{128,192},{192,128},{256,320},{320,256},{384,448},{4... | collective-permute-start | bytes 2359304 | tf_op jit(solution)/shard_map/ppermute | solution.py:420

commit v5 on v4

--- a/solution.py
+++ b/solution.py
@@ -13,7 +13,7 @@
 NT = (((1,), (1,)), ((), ()))
 MIB = 1 << 20
 fixed = pltpu.with_memory_space_constraint
-ROW = (5, 4, 1, 0, 7, 6, 3, 2)
+ROW = (5, 4, 1, 0, 3, 2, 7, 6)
 COL = (7, 6, 5, 4, 3, 2, 1, 0)
 SPANS = ((0, 160),)
 

time: 96.8 us -> 96.6 us (level)
  waiting for transfers between devices: 16.1 us -> 18.6 us
  blocking collectives: 49.4 us -> 47.7 us
    all_to_all x1, waiting for transfers between devices: 15.6 us -> 17.6 us  [local(): lax.all_to_all(sent, 'row', split_axis=0, concat_axis=0, tiled=True, axis...]
    all_to_all x1, blocking collectives: 49.4 us -> 47.7 us  [local(): lax.all_to_all(result, 'col', split_axis=0, concat_axis=0, tiled=True, ax...]
where the time goes in v5:
time: 96.6 us; the launch traced here: 96 us
  blocking collectives  47.7 us (49%)
  waiting for transfers between devices  18.6 us (19%)
  starting transfers between devices  15.5 us (16%)
  Pallas kernels  11.7 us (12%)
  local copies, waits for them, and re-layouts  1.82 us (2%)
    all_to_all x1, blocking collectives, local(): lax.all_to_all(result, 'col', split_axis=0, concat_axis=0, tiled=True, ax...  47.7 us
    all_to_all x1, waiting for transfers between devices, local(): lax.all_to_all(sent, 'row', split_axis=0, concat_axis=0, tiled=True, axis...  17.6 us
    all_to_all x1, starting transfers between devices, local(): lax.all_to_all(sent, 'row', split_axis=0, concat_axis=0, tiled=True, axis...  13.6 us
    pallas_call x1, Pallas kernels, build_weights(): pl.pallas_call(weights_kernel, out_shape=(jax.ShapeDtypeStruct((2, size,...  3.04 us
    pallas_call x1, Pallas kernels, pack(): pl.pallas_call(pack_kernel, out_shape=jax.ShapeDtypeStruct((line // 128,...  2.88 us
    pallas_call x1, Pallas kernels, compact(): pl.pallas_call(compact_kernel, out_shape=(jax.ShapeDtypeStruct((1024, 384...  2.21 us
  transfers between devices with their start and end apart: 2, of which 2 were waited for; matrix products, arithmetic and copies ran while one was open for 0% of the time, Pallas kernels for 5%

profile of v5, /device:TPU:1, one launch (start us, length us, event | category | flops | bytes accessed | tf_op | source)
XLA Modules:
  0.0 96.0 jit_solution(15155987026034164432)
XLA Ops:
  0.6 2.9 %shard_map.68 = bf16[8,512,128]{2,1,0:T(8,128)(2,1)} custom-call(bf16[3,160,1024]{2,1,0:T(8,128)(2,1)} %bitcast.5, f32[4,256,256]{2,1,0:T(8,128)} %inv_x.1), custom_call_target="tpu_custom_call" | custom-call | tf_op jit(solution)/shard_map/pallas_call | solution.py:172
  3.5 0.0 copy-start
  3.5 0.0 copy-start.2
  3.5 0.0 copy-start.4
  3.6 13.6 %all-to-all-start = ((bf16[8,512,128]{2,1,0:T(8,128)(2,1)}), bf16[8,512,128]{2,1,0:T(8,128)(2,1)S(1)}, u32[]{:S(2)}, u32[]{:S(2)}) async-start(bf16[8,512,128]{2,1,0:T(8,128)(2,1)} %shard_map.68), calls=%async_computation | async-start | bytes 2097152 | tf_op jit(solution)/shard_map/all_to_all | solution.py:415
  17.1 0.0 copy-start.5
  17.1 0.1 pad_add_fusion.where
  17.2 0.0 copy-done
  17.2 0.0 copy-done.2
  17.2 0.0 copy-done.4
  17.2 3.0 %shard_map.69 = (bf16[2,1024,384]{2,1,0:T(8,128)(2,1)S(1)}, bf16[64,1024]{1,0:T(8,128)(2,1)S(1)}, bf16[256,640]{1,0:T(8,128)(2,1)S(1)}) custom-call(s32[2]{0:T(128)S(1)} %pad_add_fusion.where, f32[4,256,256]{2,1,0:T(8,128)S(1)} %copy-done, f32[4,256,256]{2,1,0:T(8,128)S(1)} %copy-done.2, f32[8,128]{1,0:T(8,128)S(1)} %bitcast.4), custom_call_target="tpu_custom_call" | custom-call | flops 20000000 | bytes 6000000 | tf_op jit(solution)/shard_map/pallas_call | solution.py:222
  20.2 0.0 copy-start.1
  20.2 1.1 %copy-done.1 = bf16[2,1024,384]{2,1,0:T(8,128)(2,1)} copy-done((bf16[2,1024,384]{2,1,0:T(8,128)(2,1)}, bf16[2,1024,384]{2,1,0:T(8,128)(2,1)S(1)}, u32[]{:S(2)}) %copy-start.1) | copy-done | bytes 1572888
  21.4 0.0 copy-start.3
  21.4 0.7 copy-done.3
  22.0 17.6 %all-to-all-done.recv = bf16[8,512,128]{2,1,0:T(8,128)(2,1)S(1)} async-done(((bf16[8,512,128]{2,1,0:T(8,128)(2,1)}), bf16[8,512,128]{2,1,0:T(8,128)(2,1)S(1)}, u32[]{:S(2)}, u32[]{:S(2)}) %all-to-all-start) | async-done | bytes 1048608 | tf_op jit(solution)/shard_map/all_to_all | solution.py:415
  39.7 0.0 copy-done.5
  39.7 2.2 %shard_map.70 = (bf16[1024,384]{1,0:T(8,128)(2,1)S(1)}, bf16[1024,128]{1,0:T(8,128)(2,1)S(1)}, bf16[2,1024,384]{2,1,0:T(8,128)(2,1)S(1)}, bf16[64,1024]{1,0:T(8,128)(2,1)S(1)}) custom-call(s32[1,8]{1,0:T(1,128)S(1)} %copy-done.5, bf16[8,512,128]{2,1,0:T(8,128)(2,1)S(1)} %all-to-all-done.recv, bf16[2,1024,384]{2,1,0:T(8,128)(2,1)} %copy-done.1, ...), custom_call_target="tpu_custom_call" | custom-call | tf_op jit(solution)/shard_map/pallas_call | solution.py:311
  41.9 1.9 %collective-permute-start = (bf16[1024,384]{1,0:T(8,128)(2,1)S(1)}, bf16[1024,384]{1,0:T(8,128)(2,1)S(1)}, u32[]{:S(2)}, u32[]{:S(2)}) collective-permute-start(bf16[1024,384]{1,0:T(8,128)(2,1)S(1)} %get-tuple-element.19.packed), channel_id=1, source_target_pairs={{0,64},{64,0},{128,192},{192,128},{256,320},{320,256},{384,448},{4... | collective-permute-start | bytes 2359304 | tf_op jit(solution)/shard_map/ppermute | solution.py:420
  43.8 1.3 %shard_map.71.sent = bf16[64,48,128]{2,1,0:T(8,128)(2,1)S(1)} custom-call(bf16[1024,384]{1,0:T(8,128)(2,1)S(1)} %get-tuple-element.19.packed, bf16[2,1024,384]{2,1,0:T(8,128)(2,1)S(1)} %get-tuple-element.22.weights, bf16[64,1024]{1,0:T(8,128)(2,1)S(1)} %get-tuple-element.23.rows), custom_call_target="tpu_custom_call" | custom-call | flops 1600000000 | bytes 6000000 | tf_op jit(solution)/shard_map/pallas_call | solution.py:345
  45.2 0.9 collective-permute-done.partner
  46.1 1.1 %shard_map.72 = bf16[64,96,128]{2,1,0:T(8,128)(2,1)S(1)} custom-call(bf16[1024,384]{1,0:T(8,128)(2,1)S(1)} %get-tuple-element.19.packed, bf16[1024,384]{1,0:T(8,128)(2,1)S(1)} %collective-permute-done.partner, bf16[1024,128]{1,0:T(8,128)(2,1)S(1)} %get-tuple-element.20.extras, bf16[256,640]{1,0:T(8,128)(2,1)S(1)} %get-tuple-element.21.weights, ...), custom_call_target="tpu_custom_call" | custom-call | tf_op jit(solution)/shard_map/pallas_call | solution.py:373
  47.1 47.7 %all_to_all.10.recv = bf16[64,96,128]{2,1,0:T(8,128)(2,1)S(1)} all-to-all(bf16[64,96,128]{2,1,0:T(8,128)(2,1)S(1)} %shard_map.72), channel_id=1, replica_groups={{56,57,58,59,60,61,62,63,48,49,50,51,52,53,54,55,40,41,42,43,44,45,46,4..., dimensions={0} | all-to-all | bytes 3145728 | tf_op jit(solution)/shard_map/all_to_all | solution.py:423
  94.8 1.2 %shard_map.73 = (bf16[3,64,16,128]{3,2,1,0:T(8,128)(2,1)}, bf16[3,64,16,128]{3,2,1,0:T(8,128)(2,1)}) custom-call(bf16[64,96,128]{2,1,0:T(8,128)(2,1)S(1)} %all_to_all.10.recv), custom_call_target="tpu_custom_call" | custom-call | tf_op jit(solution)/shard_map/pallas_call | solution.py:400
Async XLA Ops:
  3.5 13.7 %copy-start = (f32[4,256,256]{2,1,0:T(8,128)S(1)}, f32[4,256,256]{2,1,0:T(8,128)}, u32[]{:S(2)}) copy-start(f32[4,256,256]{2,1,0:T(8,128)} %inv_x.1) | copy-start | bytes 3145732
  3.5 13.7 %copy-start.2 = (f32[4,256,256]{2,1,0:T(8,128)S(1)}, f32[4,256,256]{2,1,0:T(8,128)}, u32[]{:S(2)}) copy-start(f32[4,256,256]{2,1,0:T(8,128)} %inv_y.1) | copy-start | bytes 3145732
  3.5 13.6 %copy-start.4 = (f32[1024]{0:T(1024)S(1)}, f32[1024]{0:T(1024)}, u32[]{:S(2)}) copy-start(f32[1024]{0:T(1024)} %param.9) | copy-start | bytes 12292
  3.6 36.1 %all-to-all-start = ((bf16[8,512,128]{2,1,0:T(8,128)(2,1)}), bf16[8,512,128]{2,1,0:T(8,128)(2,1)S(1)}, u32[]{:S(2)}, u32[]{:S(2)}) async-start(bf16[8,512,128]{2,1,0:T(8,128)(2,1)} %shard_map.68), calls=%async_computation | async-start | bytes 2097152 | tf_op jit(solution)/shard_map/all_to_all | solution.py:415
  17.1 22.6 %copy-start.5 = (s32[1,8]{1,0:T(1,128)S(1)}, s32[1,8]{1,0:T(1,128)}, u32[]{:S(2)}) copy-start(s32[1,8]{1,0:T(1,128)} %lengths.1) | copy-start | bytes 100
  20.2 1.2 %copy-start.1 = (bf16[2,1024,384]{2,1,0:T(8,128)(2,1)}, bf16[2,1024,384]{2,1,0:T(8,128)(2,1)S(1)}, u32[]{:S(2)}) copy-start(bf16[2,1024,384]{2,1,0:T(8,128)(2,1)S(1)} %get-tuple-element.17.weights_hbm) | copy-start | bytes 4718596
  21.4 0.7 copy-start.3
  41.9 4.2 %collective-permute-start = (bf16[1024,384]{1,0:T(8,128)(2,1)S(1)}, bf16[1024,384]{1,0:T(8,128)(2,1)S(1)}, u32[]{:S(2)}, u32[]{:S(2)}) collective-permute-start(bf16[1024,384]{1,0:T(8,128)(2,1)S(1)} %get-tuple-element.19.packed), channel_id=1, source_target_pairs={{0,64},{64,0},{128,192},{192,128},{256,320},{320,256},{384,448},{4... | collective-permute-start | bytes 2359304 | tf_op jit(solution)/shard_map/ppermute | solution.py:420
